TPU v7x, 128 devices: a whole 4x4x4 slice. The times are simulated.
128 devices in a mesh: dp: 8 (over z, x_lo), graph: 16 (over x_hi, y, core).
Axes of the slice: x: 4 (x_hi: 2, x_lo: 2; x = x_hi * 2 + x_lo), y: 4, z: 4, core: 2. Of those that a mesh axis runs over, the one named last changes fastest.
Arguments:
- node_feat: bfloat16 [8, 384, 6272], P('dp', 'graph'), may hold values from -6 to 6
- radial: bfloat16 [8, 12288, 128], P('dp', 'graph'), may hold values from -6 to 6
- src_node: int32 [8, 12288], P('dp', 'graph'), may hold values from 0 to 383, as said below
- dst_node: int32 [8, 12288], P('dp', 'graph'), may hold values from 0 to 383, as said below
- w_query: bfloat16 [128, 128], replicated, may hold values from -0.5 to 0.5
- w_key: bfloat16 [128, 128], replicated, may hold values from -0.5 to 0.5
- w_radial: bfloat16 [128, 896], replicated, may hold values from -0.5 to 0.5
- w_degree: bfloat16 [7, 128, 128], replicated, may hold values from -0.5 to 0.5
- cotangent: bfloat16 [8, 384, 6272], P('dp', 'graph'), may hold values from -6 to 6
Outputs:
- updated: bfloat16 [8, 384, 6272], P('dp', 'graph')
- grad_node: bfloat16 [8, 384, 6272], P('dp', 'graph')
- grad_query: float32 [128, 128], replicated
- grad_key: float32 [128, 128], replicated
- grad_radial: float32 [128, 896], replicated
- grad_degree: float32 [7, 128, 128], replicated
Inputs may be any that keep to these rules, and one draw needn't show every extreme that they name: `src_node`: any atom of the structure. `dst_node`: edges at positions k * 768 to (k + 1) * 768 - 1 target atoms k * 24 to (k + 1) * 24 - 1.
All inputs are finite; a program needn't handle non-finite values.
Results may differ from a plain program's by a relative error of at most 0.015.
Values may be sent and summed in bfloat16 or wider, within the bound.
A program may use at most 256 MiB of HBM per device.

v0:
```python
import math

import jax
import jax.numpy as jnp
import numpy as np
from jax import lax
from jax.sharding import PartitionSpec as P

HEADS = 8


def degree_of(count):
    return np.floor(np.sqrt(np.arange(count) + 0.5)).astype(np.int32)


def per_degree(block_fn, packed, levels, channels):
    pieces = []
    for degree in range(levels):
        first_col = degree * degree * channels
        last_col = (degree + 1) * (degree + 1) * channels
        row_block = packed[:, first_col:last_col].reshape(-1, channels)
        pieces.append(block_fn(degree, row_block).reshape(packed.shape[0], -1))
    return jnp.concatenate(pieces, axis=1)


def on_device(node_feat, radial, src_node, dst_node, w_query, w_key, w_radial, w_degree, cotangent):
    own_nodes = node_feat[0]
    radial_rows = radial[0]
    sources = src_node[0]
    targets = dst_node[0]
    upstream = cotangent[0]
    node_count = own_nodes.shape[0]
    channels = w_query.shape[0]
    levels = w_degree.shape[0]
    coeffs = levels * levels
    packed_width = coeffs * channels
    edge_count = sources.shape[0]
    head_size = channels // HEADS
    logit_scale = 1.0 / math.sqrt(head_size)
    highest = lax.Precision.HIGHEST
    table = degree_of(coeffs)
    fold_table = jnp.asarray((table[:, None] == np.arange(levels)[None, :]).astype(np.float32))
    local_dst = targets - lax.axis_index("graph") * node_count
    dst_hot = local_dst[:, None] == jnp.arange(node_count, dtype=jnp.int32)[None, :]
    dst_half = dst_hot.astype(jnp.bfloat16)
    dst_float = dst_hot.astype(jnp.float32)
    contract_rows = (((0,), (0,)), ((), ()))

    def pick_rows(gathered):
        src_hot = (
            sources[:, None] == jnp.arange(gathered.shape[0], dtype=jnp.int32)[None, :]
        ).astype(jnp.bfloat16)
        return jnp.dot(src_hot, gathered, preferred_element_type=jnp.float32).astype(jnp.bfloat16)

    query = jnp.dot(own_nodes[:, :channels], w_query, preferred_element_type=jnp.float32)
    query_edge = jnp.take(query, local_dst, axis=0)
    pre_gate = jnp.dot(radial_rows, w_radial, preferred_element_type=jnp.float32)
    gate_full = jax.nn.silu(pre_gate).reshape(edge_count, levels, channels)[:, table, :]

    def attend(edge_rows):
        key_edge = jnp.dot(edge_rows[:, :channels], w_key, preferred_element_type=jnp.float32)
        logits = (query_edge * key_edge).reshape(edge_count, HEADS, head_size).sum(-1) * logit_scale
        attention = jax.nn.sigmoid(logits)
        return (key_edge, attention, jnp.repeat(attention, head_size, axis=1))

    edge_x = pick_rows(lax.all_gather(own_nodes, "graph", axis=0, tiled=True))
    key_edge, attention, attn_full = attend(edge_x)
    edge_x3 = edge_x.reshape(edge_count, coeffs, channels).astype(jnp.float32)
    message = (
        (edge_x3 * gate_full * attn_full[:, None, :])
        .astype(jnp.bfloat16)
        .reshape(edge_count, packed_width)
    )
    gathered_sum = lax.dot_general(
        dst_half, message, contract_rows, preferred_element_type=jnp.float32
    ).astype(jnp.bfloat16)
    mixed = per_degree(
        lambda degree, row_block: jnp.dot(
            row_block, w_degree[degree], preferred_element_type=jnp.float32
        ),
        gathered_sum,
        levels,
        channels,
    )
    updated = (own_nodes.astype(jnp.float32) + mixed).astype(jnp.bfloat16)
    degree_grads = []
    for degree in range(levels):
        first_col = degree * degree * channels
        last_col = (degree + 1) * (degree + 1) * channels
        left_rows = gathered_sum[:, first_col:last_col].reshape(-1, channels)
        right_rows = upstream[:, first_col:last_col].reshape(-1, channels)
        degree_grads.append(jnp.dot(left_rows.T, right_rows, preferred_element_type=jnp.float32))
    grad_degree_local = jnp.stack(degree_grads)
    upstream_sum = per_degree(
        lambda degree, row_block: jnp.dot(
            row_block, w_degree[degree].T, preferred_element_type=jnp.float32
        ),
        upstream,
        levels,
        channels,
    ).astype(jnp.bfloat16)
    edge_grad = jnp.dot(dst_half, upstream_sum, preferred_element_type=jnp.float32).reshape(
        edge_count, coeffs, channels
    )
    again_x = pick_rows(lax.all_gather(own_nodes, "graph", axis=0, tiled=True))
    again3 = again_x.reshape(edge_count, coeffs, channels).astype(jnp.float32)
    key_again, attention_again, attn_again = attend(again_x)
    grad_gate = jnp.einsum(
        "ekc,kl->elc", edge_grad * again3 * attn_again[:, None, :], fold_table, precision=highest
    )
    grad_attn = jnp.sum(edge_grad * again3 * gate_full, axis=1)
    grad_logit = (
        grad_attn.reshape(edge_count, HEADS, head_size).sum(-1)
        * attention_again
        * (1.0 - attention_again)
        * logit_scale
    )
    logit_full = jnp.repeat(grad_logit, head_size, axis=1)
    grad_key_edge = logit_full * query_edge
    grad_query_edge = logit_full * key_again
    grad_key_local = jnp.dot(
        again_x[:, :channels].astype(jnp.float32).T, grad_key_edge, precision=highest
    )
    query_node = jnp.dot(dst_float.T, grad_query_edge, precision=highest)
    grad_query_local = jnp.dot(
        own_nodes[:, :channels].astype(jnp.float32).T, query_node, precision=highest
    )
    sigma = jax.nn.sigmoid(pre_gate)
    grad_pre = (
        grad_gate.reshape(edge_count, levels * channels) * sigma * (1.0 + pre_gate * (1.0 - sigma))
    )
    grad_radial_local = jnp.dot(radial_rows.astype(jnp.float32).T, grad_pre, precision=highest)
    edge_back = (edge_grad * gate_full * attn_again[:, None, :]).reshape(edge_count, packed_width)
    key_back = jnp.dot(grad_key_edge, w_key.astype(jnp.float32).T, precision=highest)
    edge_back = jnp.concatenate(
        [edge_back[:, :channels] + key_back, edge_back[:, channels:]], axis=1
    ).astype(jnp.bfloat16)
    src_hot = (
        sources[:, None]
        == jnp.arange(node_count * lax.axis_size("graph"), dtype=jnp.int32)[None, :]
    ).astype(jnp.bfloat16)
    spread = lax.psum_scatter(
        lax.dot_general(
            src_hot, edge_back, contract_rows, preferred_element_type=jnp.float32
        ).astype(jnp.bfloat16),
        "graph",
        scatter_dimension=0,
        tiled=True,
    ).astype(jnp.float32)
    query_back = jnp.dot(query_node, w_query.astype(jnp.float32).T, precision=highest)
    grad_own = upstream.astype(jnp.float32) + spread
    grad_own = jnp.concatenate(
        [grad_own[:, :channels] + query_back, grad_own[:, channels:]], axis=1
    ).astype(jnp.bfloat16)
    summed = lax.psum(
        (grad_query_local, grad_key_local, grad_radial_local, grad_degree_local), ("dp", "graph")
    )
    return (updated[None], grad_own[None], summed[0], summed[1], summed[2], summed[3])


def solution(mesh):
    return jax.shard_map(
        on_device,
        mesh=mesh,
        in_specs=(
            P("dp", "graph", None),
            P("dp", "graph", None),
            P("dp", "graph"),
            P("dp", "graph"),
            P(),
            P(),
            P(),
            P(),
            P("dp", "graph", None),
        ),
        out_specs=(P("dp", "graph", None), P("dp", "graph", None), P(), P(), P(), P()),
        check_vma=False,
    )
```

profile of v0, /device:TPU:1, one launch (start us, length us, event | category | flops | bytes accessed | tf_op | source)
XLA Modules:
  0.0 552.6 jit_solution(1654223478698974391)
XLA Ops:
  8.0 1.3 slice.148
  9.3 1.4 slice.149
  10.7 1.4 slice.150
  12.1 1.4 slice.151
  13.5 0.9 slice.152
  14.4 0.9 slice.153
  16.7 0.9 fusion.90
  17.6 1.6 gather_fusion.1
  19.3 3.3 fusion.17
  22.6 2.2 copy.37
  24.9 2.2 copy.38
  27.1 8.4 %gather_fusion = f32[49,768,128]{2,1,0:T(8,128)} fusion(f32[768,7,128]{2,0,1:T(8,128)S(1)} %copy.38, s32[1024]{0:T(1024)S(1)} %get-tuple-element.37), kind=kCustom, calls=%fused_computation | custom fusion | bytes 38535364 | tf_op jit(solution)/shard_map/gather | solution.py:58
  35.4 19.5 %copy.39 = f32[768,49,128]{0,2,1:T(8,128)} copy(f32[768,49,128]{2,0,1:T(8,128)} %bitcast.146) | data formatting | bytes 38535168 | tf_op jit(solution)/shard_map/gather | solution.py:58
  55.0 19.7 %copy.40 = f32[768,6272]{1,0:T(8,128)} copy(f32[768,6272]{0,1:T(8,128)} %bitcast.149) | data formatting | bytes 38535168 | tf_op jit(solution)/shard_map/gather | solution.py:58
  77.9 8.0 %convolution_convert_fusion = bf16[768,6272]{1,0:T(8,128)(2,1)S(1)} fusion(bf16[1,384,6272]{2,1,0:T(8,128)(2,1)} %all-gather.3.cloned.1.call-done, s32[768]{0:T(1024)S(1)} %reduce.1), kind=kOutput, calls=%fused_computation.9 | convolution fusion | flops 3704487936 | bytes 14453760 | tf_op jit(solution)/shard_map/dot_general | solution.py:53
  86.0 3.5 copy-done.3
  89.9 8.7 %mul.89 = f32[768,49,128]{0,2,1:T(8,128)} broadcast(f32[768,128]{0,1:T(8,128)S(1)} %bitcast.153), dimensions={0,2} | broadcast | bytes 19660800 | tf_op jit(solution)/shard_map/mul | solution.py:70
  98.6 19.5 %copy.42 = f32[768,6272]{1,0:T(8,128)} copy(f32[768,6272]{0,1:T(8,128)} %bitcast.150) | data formatting | bytes 38535168 | tf_op jit(solution)/shard_map/mul | solution.py:70
  118.1 16.1 %fusion.7 = bf16[24,6272]{1,0:T(8,128)(2,1)S(1)} fusion(f32[768,6272]{1,0:T(8,128)} %copy.42, f32[768,6272]{1,0:T(8,128)} %copy.40, bf16[768,6272]{1,0:T(8,128)(2,1)} %copy-done.3, s32[768]{0:T(1024)S(1)} %subtract_reduce_fusion), kind=kOutput, calls=%fused_computation.16 | convolution fusion | flops 250647552 | bytes 48473088 | tf_op jit(solution)/shard_map/dot_general | solution.py:74
  134.3 1.5 fusion.29
  135.8 29.8 %convert_multiply_fusion = (f32[768,6272]{1,0:T(8,128)}, f32[768,6272]{1,0:T(8,128)}) fusion(bf16[768,6272]{1,0:T(8,128)(2,1)} %copy-done.3, f32[768,6272]{1,0:T(8,128)} %copy.42, f32[768,6272]{1,0:T(8,128)} %copy.40, bf16[24,6272]{1,0:T(8,128)(2,1)S(1)} %constant_dynamic-update-slice_fusion.6, s32[768]{0:T(1024)S(1)} %subtract_reduce_fusion), kind=kOutput, calls=%fused_computation.2 | convolution fusion | flops 250497024 | bytes 87008256 | tf_op jit(solution)/shard_map/dot_general | solution.py:102
  165.7 19.5 %copy.45 = f32[768,6272]{0,1:T(8,128)} copy(f32[768,6272]{1,0:T(8,128)} %get-tuple-element.28) | data formatting | bytes 38535168 | tf_op jit(solution)/shard_map/mul | solution.py:111
  185.2 19.5 %copy.46 = f32[768,49,128]{2,0,1:T(8,128)} copy(f32[768,49,128]{0,2,1:T(8,128)} %bitcast.147) | data formatting | bytes 38535168 | tf_op jit(solution)/shard_map/mul | solution.py:111
  204.6 14.9 %broadcast_multiply_fusion = f32[768,49,128]{0,2,1:T(8,128)} fusion(f32[768,49,128]{0,2,1:T(8,128)} %bitcast.148, f32[768,128]{0,1:T(8,128)S(1)} %bitcast.154), kind=kLoop, calls=%fused_computation.15 | loop fusion | flops 4816896 | bytes 38928384 | tf_op jit(solution)/shard_map/mul | solution.py:109
  219.5 4.1 copy-done.2
  223.6 8.1 %multiply_reduce_fusion = f32[768,128]{1,0:T(8,128)S(1)} fusion(f32[768,49,128]{2,0,1:T(8,128)S(1)} %copy-done.2, f32[49,768,128]{2,1,0:T(8,128)} %gather_fusion), kind=kLoop, calls=%fused_computation.6 | loop fusion | flops 9535488 | bytes 38928384 | tf_op jit(solution)/shard_map/reduce_sum | solution.py:111
  232.1 1.9 fusion.47
  234.0 2.2 fusion.22
  236.2 10.0 %slice.236 = bf16[768,6144]{1,0:T(8,128)(2,1)} slice(f32[768,6272]{1,0:T(8,128)} %get-tuple-element.29), slice={[0:768], [128:6272]} | slice | bytes 18874368 | tf_op jit(solution)/shard_map/slice | solution.py:136
  249.1 1.6 convolution_bitcast_fusion.8
  250.6 19.1 %copy.49 = f32[768,49,128]{2,1,0:T(8,128)} copy(f32[768,49,128]{0,2,1:T(8,128)} %broadcast_multiply_fusion) | data formatting | bytes 38535168 | tf_op jit(solution)/shard_map/mul | solution.py:109
  269.8 16.0 %convolution_bitcast_fusion = f32[768,7,128]{2,1,0:T(8,128)S(1)} fusion(f32[768,49,128]{2,1,0:T(8,128)} %copy.49, f32[49,7,1]{0,1,2:T(8,128)S(1)} %copy-done.33), kind=kOutput, calls=%fused_computation.26 | convolution fusion | flops 404619264 | bytes 22021468 | tf_op jit(solution)/shard_map/ekc,kl->elc/dot_general | solution.py:108
  285.8 2.3 copy.50
  288.1 2.4 copy.51
  291.4 1.6 fusion.27
  293.0 1.6 fusion.26
  294.6 1.6 fusion.25
  296.3 0.8 fusion.24
  297.1 0.8 fusion.23
  298.0 5.4 fusion.19
  303.5 10.1 %convolution_convert_fusion.1 = bf16[384,6272]{1,0:T(8,128)(2,1)} fusion(bf16[768,6144]{1,0:T(8,128)(2,1)} %slice.236, bf16[768,128]{1,0:T(8,128)(2,1)S(1)} %copy-done.22, s32[768]{0:T(1024)S(1)} %reduce.1), kind=kOutput, calls=%fused_computation.10 | convolution fusion | flops 3721347072 | bytes 14453760 | tf_op jit(solution)/shard_map/dot_general | solution.py:143
  315.9 139.4 %all-reduce.4.cloned.1.call-done = (f32[128,128]{0,1:T(8,128)}, f32[128,128]{1,0:T(8,128)}, f32[128,896]{0,1:T(8,128)}, f32[7,128,128]{2,1,0:T(8,128)}) async-done(((f32[128,128]{0,1:T(8,128)}, f32[128,128]{1,0:T(8,128)}, f32[128,896]{0,1:T(8,128)}, f32[7,128,128]{2,1,0:T(8,128)}), (f32[128,128]{0,1:T(8,128)}, f32[128,128]{1,0:T(8,128)}, f32[128,896]{0,1:T(8,128)}, ...) | async-done | bytes 1048592 | tf_op jit(solution)/shard_map/psum | solution.py:155
  455.2 2.0 copy.53
  457.2 1.6 copy.52
  458.8 82.0 %reduce-scatter.4.cloned.1.call-done = bf16[24,6272]{1,0:T(8,128)(2,1)} async-done(((bf16[384,6272]{1,0:T(8,128)(2,1)}), bf16[24,6272]{1,0:T(8,128)(2,1)}) %reduce-scatter.4.cloned.1.call-update) | async-done | bytes 301072
  540.8 1.0 convert_add_fusion
  542.8 1.5 copy.77
  544.3 1.8 copy.78
  (156 shorter events, 12.7 us)
Async XLA Ops:
  7.2 12.1 %copy-start = (bf16[128,896]{1,0:T(8,128)(2,1)S(1)}, bf16[128,896]{1,0:T(8,128)(2,1)}, u32[]{:S(2)}) copy-start(bf16[128,896]{1,0:T(8,128)(2,1)} %param.18) | copy-start | bytes 688132
  7.2 70.8 %all-gather.3.cloned.1.call-start = ((), (), s32[]{:S(2)}) async-start(), calls=%async_computation.1 | async-start | bytes 5117952 | tf_op jit(solution)/shard_map/all_gather | solution.py:66
  7.9 447.3 %all-reduce.4.cloned.1.call-start = ((), (), s32[]{:S(2)}) async-start(), calls=%async_computation.3 | async-start | bytes 2097152 | tf_op jit(solution)/shard_map/psum | solution.py:155
  55.0 19.8 %copy-start.31 = (bf16[24,384]{1,0:T(8,128)(2,1)S(1)}, bf16[24,384]{1,0:T(8,128)(2,1)}, u32[]{:S(2)}) copy-start(bf16[24,384]{1,0:T(8,128)(2,1)} %slice.148) | copy-start | bytes 55300
  55.0 19.8 %copy-start.28 = (bf16[24,640]{1,0:T(8,128)(2,1)S(1)}, bf16[24,640]{1,0:T(8,128)(2,1)}, u32[]{:S(2)}) copy-start(bf16[24,640]{1,0:T(8,128)(2,1)} %slice.149) | copy-start | bytes 92164
  55.0 19.8 %copy-start.23 = (bf16[24,896]{1,0:T(8,128)(2,1)S(1)}, bf16[24,896]{1,0:T(8,128)(2,1)}, u32[]{:S(2)}) copy-start(bf16[24,896]{1,0:T(8,128)(2,1)} %slice.150) | copy-start | bytes 129028
  55.0 19.9 %copy-start.21 = (bf16[24,1152]{1,0:T(8,128)(2,1)S(1)}, bf16[24,1152]{1,0:T(8,128)(2,1)}, u32[]{:S(2)}) copy-start(bf16[24,1152]{1,0:T(8,128)(2,1)} %slice.151) | copy-start | bytes 165892
  55.0 20.3 %copy-start.8 = (bf16[7,128,128]{2,1,0:T(8,128)(2,1)S(1)}, bf16[7,128,128]{2,1,0:T(8,128)(2,1)}, u32[]{:S(2)}) copy-start(bf16[7,128,128]{2,1,0:T(8,128)(2,1)} %param.19) | copy-start | bytes 688132
  55.0 21.9 %copy-start.34 = (s32[1,768]{1,0:T(1,128)S(1)}, s32[1,768]{1,0:T(1,128)}, u32[]{:S(2)}) copy-start(s32[1,768]{1,0:T(1,128)} %param.14) | copy-start | bytes 9220
  55.0 21.9 %copy-start.32 = (s32[1,768]{1,0:T(1,128)S(1)}, s32[1,768]{1,0:T(1,128)}, u32[]{:S(2)}) copy-start(s32[1,768]{1,0:T(1,128)} %param.15) | copy-start | bytes 9220
  74.8 1.7 copy-start.19
  74.9 11.0 %copy-start.18 = (bf16[168,128]{1,0:T(8,128)(2,1)}, bf16[168,128]{1,0:T(8,128)(2,1)S(1)}, u32[]{:S(2)}) copy-start(bf16[168,128]{1,0:T(8,128)(2,1)S(1)} %reshape.207) | copy-start | bytes 129028
  75.0 10.9 %copy-start.14 = (bf16[216,128]{1,0:T(8,128)(2,1)}, bf16[216,128]{1,0:T(8,128)(2,1)S(1)}, u32[]{:S(2)}) copy-start(bf16[216,128]{1,0:T(8,128)(2,1)S(1)} %reshape.209) | copy-start | bytes 165892
  75.1 10.8 %copy-start.12 = (bf16[264,128]{1,0:T(8,128)(2,1)}, bf16[264,128]{1,0:T(8,128)(2,1)S(1)}, u32[]{:S(2)}) copy-start(bf16[264,128]{1,0:T(8,128)(2,1)S(1)} %reshape.211) | copy-start | bytes 202756
  75.3 10.7 %copy-start.10 = (bf16[312,128]{1,0:T(8,128)(2,1)}, bf16[312,128]{1,0:T(8,128)(2,1)S(1)}, u32[]{:S(2)}) copy-start(bf16[312,128]{1,0:T(8,128)(2,1)S(1)} %reshape.213) | copy-start | bytes 239620
  76.6 13.0 %copy-start.26 = (bf16[128,128]{1,0:T(8,128)(2,1)S(1)}, bf16[128,128]{1,0:T(8,128)(2,1)}, u32[]{:S(2)}) copy-start(bf16[128,128]{1,0:T(8,128)(2,1)} %param.17) | copy-start | bytes 98308
  86.0 3.6 copy-start.3
  134.3 31.3 %copy-start.5 = (bf16[24,6272]{1,0:T(8,128)(2,1)}, bf16[24,6272]{1,0:T(8,128)(2,1)S(1)}, u32[]{:S(2)}) copy-start(bf16[24,6272]{1,0:T(8,128)(2,1)S(1)} %fusion.7) | copy-start | bytes 903172
  204.6 19.0 %copy-start.2 = (f32[768,49,128]{2,0,1:T(8,128)S(1)}, f32[768,49,128]{2,0,1:T(8,128)}, u32[]{:S(2)}) copy-start(f32[768,49,128]{2,0,1:T(8,128)} %copy.46) | copy-start | bytes 57802756
  236.2 10.0 %slice-start = ((bf16[24,6272]{1,0:T(8,128)(2,1)}), bf16[24,384]{1,0:T(8,128)(2,1)S(1)}, s32[]{:S(2)}) async-start(bf16[24,6272]{1,0:T(8,128)(2,1)} %copy-done.5), calls=%async_computation.4 | async-start | bytes 36864 | tf_op jit(solution)/shard_map/slice | solution.py:21
  236.2 10.0 %slice-start.1 = ((bf16[24,6272]{1,0:T(8,128)(2,1)}), bf16[24,640]{1,0:T(8,128)(2,1)S(1)}, s32[]{:S(2)}) async-start(bf16[24,6272]{1,0:T(8,128)(2,1)} %copy-done.5), calls=%async_computation.5 | async-start | bytes 61440 | tf_op jit(solution)/shard_map/slice | solution.py:21
  236.2 10.7 %slice-start.2 = ((bf16[24,6272]{1,0:T(8,128)(2,1)}), bf16[24,896]{1,0:T(8,128)(2,1)S(1)}, s32[]{:S(2)}) async-start(bf16[24,6272]{1,0:T(8,128)(2,1)} %copy-done.5), calls=%async_computation.6 | async-start | bytes 86016 | tf_op jit(solution)/shard_map/slice | solution.py:21
  236.2 11.4 %slice-start.3 = ((bf16[24,6272]{1,0:T(8,128)(2,1)}), bf16[24,1152]{1,0:T(8,128)(2,1)S(1)}, s32[]{:S(2)}) async-start(bf16[24,6272]{1,0:T(8,128)(2,1)} %copy-done.5), calls=%async_computation.7 | async-start | bytes 110592 | tf_op jit(solution)/shard_map/slice | solution.py:21
  236.2 12.1 %slice-start.4 = ((bf16[24,6272]{1,0:T(8,128)(2,1)}), bf16[24,1408]{1,0:T(8,128)(2,1)S(1)}, s32[]{:S(2)}) async-start(bf16[24,6272]{1,0:T(8,128)(2,1)} %copy-done.5), calls=%async_computation.8 | async-start | bytes 135168 | tf_op jit(solution)/shard_map/slice | solution.py:21
  236.2 12.2 %slice-start.5 = ((bf16[24,6272]{1,0:T(8,128)(2,1)}), bf16[24,1664]{1,0:T(8,128)(2,1)S(1)}, s32[]{:S(2)}) async-start(bf16[24,6272]{1,0:T(8,128)(2,1)} %copy-done.5), calls=%async_computation.9 | async-start | bytes 159744 | tf_op jit(solution)/shard_map/slice | solution.py:21
  246.2 44.4 %copy-start.24 = (bf16[72,128]{1,0:T(8,128)(2,1)}, bf16[72,128]{1,0:T(8,128)(2,1)S(1)}, u32[]{:S(2)}) copy-start(bf16[72,128]{1,0:T(8,128)(2,1)S(1)} %reshape.197) | copy-start | bytes 55300
  249.0 20.7 %copy-start.29 = (f32[24,128]{1,0:T(8,128)}, f32[24,128]{1,0:T(8,128)S(1)}, u32[]{:S(2)}) copy-start(f32[24,128]{1,0:T(8,128)S(1)} %fusion.39) | copy-start | bytes 36868
  250.6 19.1 %copy-start.33 = (f32[49,7,1]{0,1,2:T(8,128)S(1)}, f32[49,7,1]{0,1,2:T(8,128)}, u32[]{:S(2)}) copy-start(f32[49,7,1]{0,1,2:T(8,128)} %constant.52) | copy-start | bytes 4120
  285.8 8.8 %copy-start.15 = (bf16[216,128]{1,0:T(8,128)(2,1)S(1)}, bf16[216,128]{1,0:T(8,128)(2,1)}, u32[]{:S(2)}) copy-start(bf16[216,128]{1,0:T(8,128)(2,1)} %copy-done.14) | copy-start | bytes 165892
  285.8 10.4 %copy-start.13 = (bf16[264,128]{1,0:T(8,128)(2,1)S(1)}, bf16[264,128]{1,0:T(8,128)(2,1)}, u32[]{:S(2)}) copy-start(bf16[264,128]{1,0:T(8,128)(2,1)} %copy-done.12) | copy-start | bytes 202756
  285.8 11.3 %copy-start.11 = (bf16[312,128]{1,0:T(8,128)(2,1)S(1)}, bf16[312,128]{1,0:T(8,128)(2,1)}, u32[]{:S(2)}) copy-start(bf16[312,128]{1,0:T(8,128)(2,1)} %copy-done.10) | copy-start | bytes 239620
  290.6 12.9 %copy-start.22 = (bf16[768,128]{1,0:T(8,128)(2,1)S(1)}, bf16[768,128]{1,0:T(8,128)(2,1)}, u32[]{:S(2)}) copy-start(bf16[768,128]{1,0:T(8,128)(2,1)} %fusion.22) | copy-start | bytes 589828
  303.3 10.3 %copy-start.9 = (bf16[7,128,128]{2,1,0:T(8,128)(2,1)S(1)}, bf16[7,128,128]{2,1,0:T(8,128)(2,1)}, u32[]{:S(2)}) copy-start(bf16[7,128,128]{2,1,0:T(8,128)(2,1)} %param.19) | copy-start | bytes 688132
  303.4 10.3 %copy-start.25 = (bf16[72,128]{1,0:T(8,128)(2,1)S(1)}, bf16[72,128]{1,0:T(8,128)(2,1)}, u32[]{:S(2)}) copy-start(bf16[72,128]{1,0:T(8,128)(2,1)} %copy-done.24) | copy-start | bytes 55300
  303.4 10.4 %copy-start.20 = (bf16[120,128]{1,0:T(8,128)(2,1)S(1)}, bf16[120,128]{1,0:T(8,128)(2,1)}, u32[]{:S(2)}) copy-start(bf16[120,128]{1,0:T(8,128)(2,1)} %reshape.198) | copy-start | bytes 92164
  303.4 10.6 %copy-start.17 = (bf16[168,128]{1,0:T(8,128)(2,1)S(1)}, bf16[168,128]{1,0:T(8,128)(2,1)}, u32[]{:S(2)}) copy-start(bf16[168,128]{1,0:T(8,128)(2,1)} %reshape.199) | copy-start | bytes 129028
  303.4 10.8 %copy-start.16 = (bf16[216,128]{1,0:T(8,128)(2,1)S(1)}, bf16[216,128]{1,0:T(8,128)(2,1)}, u32[]{:S(2)}) copy-start(bf16[216,128]{1,0:T(8,128)(2,1)} %reshape.200) | copy-start | bytes 165892
  303.4 11.4 %copy-start.6 = (bf16[24,6272]{1,0:T(8,128)(2,1)S(1)}, bf16[24,6272]{1,0:T(8,128)(2,1)}, u32[]{:S(2)}) copy-start(bf16[24,6272]{1,0:T(8,128)(2,1)} %copy-done.5) | copy-start | bytes 903172
  303.4 11.7 %copy-start.4 = (bf16[1,24,6272]{2,1,0:T(8,128)(2,1)S(1)}, bf16[1,24,6272]{2,1,0:T(8,128)(2,1)}, u32[]{:S(2)}) copy-start(bf16[1,24,6272]{2,1,0:T(8,128)(2,1)} %param.12) | copy-start | bytes 903172
  303.4 237.4 %reduce-scatter.4.cloned.1.call-start = ((), (), s32[]{:S(2)}) async-start(), calls=%async_computation.2 | async-start | bytes 5117952
  303.5 242.6 %copy-start.1 = (bf16[128,896]{1,0:T(8,128)(2,1)S(1)}, bf16[128,896]{1,0:T(8,128)(2,1)}, u32[]{:S(2)}) copy-start(bf16[128,896]{1,0:T(8,128)(2,1)} %param.18) | copy-start | bytes 688132
  313.6 227.2 %copy-start.7 = (bf16[1,24,6272]{2,1,0:T(8,128)(2,1)S(1)}, bf16[1,24,6272]{2,1,0:T(8,128)(2,1)}, u32[]{:S(2)}) copy-start(bf16[1,24,6272]{2,1,0:T(8,128)(2,1)} %param.20) | copy-start | bytes 903172
  313.6 228.2 %copy-start.27 = (bf16[128,128]{1,0:T(8,128)(2,1)S(1)}, bf16[128,128]{1,0:T(8,128)(2,1)}, u32[]{:S(2)}) copy-start(bf16[128,128]{1,0:T(8,128)(2,1)} %param.16) | copy-start | bytes 98308
  313.6 228.2 %copy-start.30 = (f32[24,128]{1,0:T(8,128)S(1)}, f32[24,128]{1,0:T(8,128)}, u32[]{:S(2)}) copy-start(f32[24,128]{1,0:T(8,128)} %copy-done.29) | copy-start | bytes 36868
Sparse Core Ops, SparseCore 0:
  10.4 61.2 all-gather.2
  303.5 151.7 all-reduce.3
  460.1 80.6 reduce-scatter.3
where the time goes:
time: 556 us; the launch traced here: 553 us
  waiting for transfers between devices  222 us (40%)
  local copies, waits for them, and re-layouts  181 us (33%)
  matrix products  108 us (19%)
  other arithmetic  27.1 us (5%)
  between operations  14.6 us (3%)
    psum x1, waiting for transfers between devices, on_device(): lax.psum((grad_query_local, grad_key_local, grad_radial_local, grad_degre...  139 us
    unnamed x4, waiting for transfers between devices  82.7 us
    gather x3, local copies, waits for them, and re-layouts, on_device(): jax.nn.silu(pre_gate).reshape(edge_count, levels, channels)[:, table, :]  47.6 us
    mul x2, local copies, waits for them, and re-layouts, on_device(): grad_attn = jnp.sum(edge_grad * again3 * gate_full, axis=1)  39 us
    dot_general x1, matrix products, on_device(): jnp.dot(dst_half, upstream_sum, preferred_element_type=jnp.float32)  29.8 us
    mul x2, local copies, waits for them, and re-layouts, on_device(): edge_x3 * gate_full * attn_full[:, None, :]  28.3 us
    mul x1, local copies, waits for them, and re-layouts, on_device(): edge_grad * again3 * attn_again[:, None, :]  19.1 us
    dot_general x1, matrix products, on_device(): lax.dot_general(dst_half, message, contract_rows, preferred_element_type=...  16.1 us
  transfers between devices with their start and end apart: 3, of which 2 were waited for; matrix products, arithmetic and copies ran while one was open for 15% of the time, Pallas kernels for 0%

commit v1 on v0

v1 whole, which is shorter than its diff:
```python
import functools
import math

import jax
import jax.numpy as jnp
from jax import lax
from jax.experimental import pallas as pl
from jax.experimental.pallas import tpu as pltpu
from jax.sharding import PartitionSpec as P

HEADS = 8
C = 128
LEVELS = 7
NODE_DEV = 24
PAD = 32
EDGE_DEV = 768
NODES = 384
CHIP_ROWS = 48
N_GRAPH = 16
N_DP = 8
HALF_PAIRS = 12
CHUNK = 2
CHUNKS = HALF_PAIRS // CHUNK
ROW_BLOCK = 256
GRAD_ROWS = 2048
GRAD_PIECE = GRAD_ROWS // N_GRAPH
MESH = pl.DeviceIdType.MESH
F32 = jnp.float32
BF16 = jnp.bfloat16

X_OWN, UP_OWN, DOWN_OWN, FAR_OWN, UP_RELAY, DOWN_RELAY, X_RELAY, TO_SIB = range(8)
SUM_SIB, PART_UP, PART_DOWN, PART_X, OWN_UP, OWN_DOWN, TOTAL_X, TOTAL_FAR, LAST_SIB = range(9)


def mm(a, b):
    return jnp.dot(a, b, preferred_element_type=F32)


def mm_nt(a, b):
    return lax.dot_general(a, b, (((1,), (1,)), ((), ())), preferred_element_type=F32)


def mm_tn(a, b):
    return lax.dot_general(a, b, (((0,), (0,)), ((), ())), preferred_element_type=F32)


def two_parts(a):
    high = a.astype(BF16)
    return high, (a - high.astype(F32)).astype(BF16)


def degree_of(k):
    total = 0
    for degree in range(1, LEVELS):
        total = total + (k + 64 - degree * degree) // 64
    return total


def columns(k, count=1):
    return pl.ds(pl.multiple_of(k * C, C), count * C)


def kernel(
    x_ref, rad_ref, src_ref, dst_ref, wq_ref, wk_ref, wr_ref, wd_ref, cot_ref,
    upd_ref, gn_ref, gw_ref,
    xs, sibx, xall, x0all, x0, src_hot, src_t, dst_hot, dst_t,
    gs, g0, gate, slope, scaled, fold, fwd, msg, back,
    part, from_sib, in_part, in_total, last, last_in, p0, in0,
    wpart, win1, win2, wall,
    qe, key, att, ex0, gm0,
    sib_sems, x0_send, x0_recv, ag_send, ag_recv, rs_send, rs_recv,
    r0_send, r0_recv, w1_send, w1_recv, w2_send, w2_recv, w3_send, w3_recv,
):
    dp = lax.axis_index("dp")
    graph = lax.axis_index("graph")
    core = lax.rem(graph, 2)
    chip = graph // 2
    x_hi = chip // 4
    y = lax.rem(chip, 4)
    other = 1 - core

    def chip_at(dx, dy):
        return lax.rem(x_hi + dx, 2) * 4 + lax.rem(y + dy, 4)

    def at(dx, dy):
        return (dp, chip_at(dx, dy) * 2 + core)

    sibling = (dp, chip * 2 + other)

    def rows_of(which):
        return pl.ds(pl.multiple_of(which * CHIP_ROWS, 16), CHIP_ROWS)

    def remote(src, dst, send, recv, device):
        return pltpu.make_async_remote_copy(
            src_ref=src, dst_ref=dst, send_sem=send, recv_sem=recv,
            device_id=device, device_id_type=MESH,
        )

    barrier = pltpu.get_barrier_semaphore()

    @pl.loop(1, N_GRAPH)
    def _(d):
        pl.semaphore_signal(
            barrier, inc=1, device_id=(dp, lax.rem(graph + d, N_GRAPH)), device_id_type=MESH
        )

    @pl.loop(1, N_DP)
    def _(d):
        pl.semaphore_signal(
            barrier, inc=1, device_id=(lax.rem(dp + d, N_DP), graph), device_id_type=MESH
        )

    for pair in range(2 * HALF_PAIRS):
        xs[pair // HALF_PAIRS, pair % HALF_PAIRS, 0:NODE_DEV, :] = x_ref[:, (1 + 2 * pair) * C : (3 + 2 * pair) * C]
        xs[pair // HALF_PAIRS, pair % HALF_PAIRS, NODE_DEV:PAD, :] = jnp.zeros((PAD - NODE_DEV, 2 * C), BF16)
    x0all[graph, 0:NODE_DEV, :] = x_ref[:, 0:C]
    x0all[graph, NODE_DEV:PAD, :] = jnp.zeros((PAD - NODE_DEV, C), BF16)

    pl.semaphore_wait(barrier, N_GRAPH - 1 + N_DP - 1)

    sib_copy = remote(xs.at[other], sibx, sib_sems.at[0], sib_sems.at[1], sibling)
    sib_copy.start()

    def x0_copy(d):
        return remote(
            x0all.at[graph], x0all.at[graph], x0_send.at[d], x0_recv.at[d],
            (dp, lax.rem(graph + d, N_GRAPH)),
        )

    @pl.loop(1, N_GRAPH)
    def _(d):
        x0_copy(d).start()

    sib_copy.wait_recv()
    mine = xs[core, :, 0:NODE_DEV, :].astype(F32)
    theirs = sibx[:, 0:NODE_DEV, :].astype(F32)
    first = jnp.where(core == 0, mine, theirs)
    second = jnp.where(core == 0, theirs, mine)
    xall[core, :, rows_of(chip), :] = jnp.concatenate([first, second], axis=1).astype(BF16)

    def block(j, which):
        return xall.at[core, pl.ds(j * CHUNK, CHUNK), rows_of(which), :]

    def gather_copy(j, kind, which, device):
        return lambda: remote(
            block(j, which), block(j, which), ag_send.at[j, kind], ag_recv.at[j, kind], device
        )

    def gather_first(j):
        return [
            gather_copy(j, X_OWN, chip, at(1, 0)),
            gather_copy(j, UP_OWN, chip, at(0, 1)),
            gather_copy(j, DOWN_OWN, chip, at(0, 3)),
            gather_copy(j, FAR_OWN, chip, at(0, 2)),
        ]

    def gather_second(j):
        return [
            gather_copy(j, UP_RELAY, chip_at(1, 0), at(0, 1)),
            gather_copy(j, DOWN_RELAY, chip_at(1, 0), at(0, 3)),
            gather_copy(j, X_RELAY, chip_at(0, 2), at(1, 0)),
        ]

    def to_sibling(j):
        ref = xall.at[core, pl.ds(j * CHUNK, CHUNK)]
        return remote(ref, ref, ag_send.at[j, TO_SIB], ag_recv.at[j, TO_SIB], sibling)

    def got_block(j, kind, which):
        gather_copy(j, kind, which, at(0, 1))().wait_recv()

    @pl.loop(0, CHUNKS)
    def _(j):
        for copy in gather_first(j):
            copy().start()

    def relay(j):
        got_block(j, X_OWN, chip_at(1, 0))
        got_block(j, FAR_OWN, chip_at(0, 2))
        for copy in gather_second(j):
            copy().start()

    def forward(j):
        got_block(j, UP_OWN, chip_at(0, 3))
        got_block(j, DOWN_OWN, chip_at(0, 1))
        got_block(j, UP_RELAY, chip_at(1, 3))
        got_block(j, DOWN_RELAY, chip_at(1, 1))
        got_block(j, X_RELAY, chip_at(1, 2))
        to_sibling(j).start()

    def from_sibling(j):
        ref = xall.at[other, pl.ds(j * CHUNK, CHUNK)]
        remote(ref, ref, ag_send.at[j, TO_SIB], ag_recv.at[j, TO_SIB], sibling).wait_recv()

    src_row = src_ref[...].astype(F32)
    dst_row = (dst_ref[...] - graph * NODE_DEV).astype(F32)
    src_t[...] = (lax.broadcasted_iota(jnp.int32, (NODES, EDGE_DEV), 0).astype(F32) == src_row).astype(F32).astype(BF16)
    dst_t[...] = (lax.broadcasted_iota(jnp.int32, (PAD, EDGE_DEV), 0).astype(F32) == dst_row).astype(F32).astype(BF16)
    src_col = jnp.broadcast_to(src_row, (8, EDGE_DEV)).T[:, 0:1]
    dst_col = jnp.broadcast_to(dst_row, (8, EDGE_DEV)).T[:, 0:1]
    src_hot[...] = (lax.broadcasted_iota(jnp.int32, (EDGE_DEV, NODES), 1).astype(F32) == src_col).astype(F32).astype(BF16)
    dst_hot[...] = (lax.broadcasted_iota(jnp.int32, (EDGE_DEV, PAD), 1).astype(F32) == dst_col).astype(F32).astype(BF16)

    for degree in range(LEVELS):
        pre = mm(rad_ref[...], wr_ref[:, degree * C : (degree + 1) * C])
        sigma = jax.nn.sigmoid(pre)
        gate[degree] = pre * sigma
        slope[degree] = sigma * (1.0 + pre * (1.0 - sigma))
        fold[degree] = jnp.zeros((EDGE_DEV, C), F32)

    zeros = jnp.zeros((PAD - NODE_DEV, C), F32)
    for degree in range(LEVELS):
        begin, end = degree * degree, (degree + 1) * (degree + 1)
        stacked = jnp.concatenate([cot_ref[:, k * C : (k + 1) * C].astype(F32) for k in range(begin, end)], axis=0)
        mixed = mm_nt(stacked.astype(BF16), wd_ref[degree])
        for k in range(begin, end):
            rows = mixed[(k - begin) * NODE_DEV : (k - begin + 1) * NODE_DEV]
            rows = jnp.concatenate([rows, zeros], axis=0).astype(BF16)
            if k == 0:
                g0[...] = rows
            else:
                lane = (k - 1) % 2
                gs[(k - 1) // 2, :, lane * C : (lane + 1) * C] = rows

    query = jnp.concatenate([mm(x_ref[:, 0:C], wq_ref[...]), zeros], axis=0)
    q_high, q_low = two_parts(query)
    qe[...] = mm(dst_hot[...], q_high) + mm(dst_hot[...], q_low)
    gm0[...] = mm(dst_hot[...], g0[...])

    head_rows = lax.broadcasted_iota(jnp.int32, (C, C), 0) // (C // HEADS)
    head_cols = lax.broadcasted_iota(jnp.int32, (C, C), 1) // (C // HEADS)
    same_head = (head_rows == head_cols).astype(F32).astype(BF16)
    scale = 1.0 / math.sqrt(C // HEADS)

    def head_sum(a):
        high, low = two_parts(a)
        return mm(high, same_head) + mm(low, same_head)

    @pl.loop(1, N_GRAPH)
    def _(d):
        x0_copy(d).wait_recv()

    x0[...] = jnp.concatenate([x0all[d, 0:NODE_DEV, :].astype(F32) for d in range(N_GRAPH)], axis=0).astype(BF16)
    relay(0)
    ex0[...] = mm(src_hot[...], x0[...]).astype(BF16)
    key[...] = mm(ex0[...], wk_ref[...])
    att[...] = jax.nn.sigmoid(head_sum(qe[...] * key[...]) * scale)
    for degree in range(LEVELS):
        scaled[degree] = gate[degree] * att[...]
    ex0_float = ex0[...].astype(F32)
    fold[0] = ex0_float * gm0[...]
    relay(1)
    forward(0)
    fwd[0] = mm(dst_t[...], (ex0_float * scaled[0]).astype(BF16))[0:NODE_DEV]

    def edges(half, t):
        pair = half * HALF_PAIRS + t
        k = 1 + 2 * pair
        left, right = degree_of(k), degree_of(k + 1)
        nodes = xall[half, t]
        ups = gs[pair]
        for begin in range(0, EDGE_DEV, ROW_BLOCK):
            rows = slice(begin, begin + ROW_BLOCK)
            ex = mm(src_hot[rows, :], nodes)
            gm = mm(dst_hot[rows, :], ups)
            for lane, degree in ((0, left), (1, right)):
                cols = slice(lane * C, (lane + 1) * C)
                factor = scaled[degree, rows, :]
                msg[rows, cols] = (ex[:, cols] * factor).astype(BF16)
                back[rows, cols] = (gm[:, cols] * factor).astype(BF16)
                fold[degree, rows, :] += ex[:, cols] * gm[:, cols]
        gathered = mm(dst_t[...], msg[...])
        fwd[k] = gathered[0:NODE_DEV, 0:C]
        fwd[k + 1] = gathered[0:NODE_DEV, C : 2 * C]
        part[half, t] = mm(src_t[...], back[...]).astype(BF16)

    def sum_sibling(j):
        return remote(
            part.at[other, pl.ds(j * CHUNK, CHUNK)], from_sib.at[pl.ds(j * CHUNK, CHUNK)],
            rs_send.at[j, SUM_SIB], rs_recv.at[j, SUM_SIB], sibling,
        )

    def part_block(j, which):
        return part.at[core, pl.ds(j * CHUNK, CHUNK), rows_of(which), :]

    def reduce_copy(j, kind, which, landing, slot, device):
        return lambda: remote(
            part_block(j, which), landing.at[slot, pl.ds(j * CHUNK, CHUNK)],
            rs_send.at[j, kind], rs_recv.at[j, kind], device,
        )

    def reduce_first(j):
        return [
            reduce_copy(j, PART_UP, chip_at(1, 1), in_part, 0, at(0, 1)),
            reduce_copy(j, PART_DOWN, chip_at(1, 3), in_part, 1, at(0, 3)),
            reduce_copy(j, PART_X, chip_at(1, 2), in_part, 2, at(1, 0)),
            reduce_copy(j, OWN_UP, chip_at(0, 1), in_total, 0, at(0, 1)),
            reduce_copy(j, OWN_DOWN, chip_at(0, 3), in_total, 1, at(0, 3)),
        ]

    def reduce_second(j):
        return [
            reduce_copy(j, TOTAL_X, chip_at(1, 0), in_total, 2, at(1, 0)),
            reduce_copy(j, TOTAL_FAR, chip_at(0, 2), in_total, 3, at(0, 2)),
        ]

    def last_copy(j):
        return remote(
            last.at[pl.ds(j * CHUNK, CHUNK), pl.ds(pl.multiple_of(other * NODE_DEV, 8), NODE_DEV), :],
            last_in.at[pl.ds(j * CHUNK, CHUNK)],
            rs_send.at[j, LAST_SIB], rs_recv.at[j, LAST_SIB], sibling,
        )

    def reduce_start(j):
        sum_sibling(j).wait_recv()
        for i in range(CHUNK):
            t = j * CHUNK + i
            part[core, t] = (part[core, t].astype(F32) + from_sib[t].astype(F32)).astype(BF16)
        for copy in reduce_first(j):
            copy().start()

    def reduce_next(j):
        for copy in reduce_first(j)[:3]:
            copy().wait_recv()
        for i in range(CHUNK):
            t = j * CHUNK + i
            rows = rows_of(chip_at(1, 0))
            total = part[core, t, rows, :].astype(F32) + in_part[0, t].astype(F32) + in_part[1, t].astype(F32)
            part[core, t, rows, :] = total.astype(BF16)
            rows = rows_of(chip_at(0, 2))
            total = part[core, t, rows, :].astype(F32) + in_part[2, t].astype(F32)
            part[core, t, rows, :] = total.astype(BF16)
        for copy in reduce_second(j):
            copy().start()

    def reduce_end(j):
        for copy in reduce_first(j)[3:] + reduce_second(j):
            copy().wait_recv()
        for i in range(CHUNK):
            t = j * CHUNK + i
            total = part[core, t, rows_of(chip), :].astype(F32)
            for slot in range(4):
                total = total + in_total[slot, t].astype(F32)
            last[t] = total
        last_copy(j).start()

    @pl.loop(0, CHUNKS)
    def _(s):
        @pl.when(s + 2 < CHUNKS)
        def _():
            relay(s + 2)

        @pl.when(s + 1 < CHUNKS)
        def _():
            forward(s + 1)

        from_sibling(s)

        @pl.loop(0, 2 * CHUNK)
        def _(i):
            half = lax.rem(other + i // CHUNK, 2)
            edges(half, s * CHUNK + lax.rem(i, CHUNK))

            @pl.when(i == CHUNK - 1)
            def _():
                sum_sibling(s).start()

        @pl.when(s >= 1)
        def _():
            reduce_start(s - 1)

        @pl.when(s >= 3)
        def _():
            reduce_next(s - 3)

        @pl.when(s >= 5)
        def _():
            reduce_end(s - 5)

    a = att[...]
    g_att = gate[0] * fold[0]
    for degree in range(1, LEVELS):
        g_att = g_att + gate[degree] * fold[degree]
    g_logit = head_sum(g_att) * a * (1.0 - a) * scale
    g_key = (g_logit * qe[...]).astype(BF16)
    q_high, q_low = two_parts(g_logit * key[...])
    back[:, 0:C] = (gm0[...] * scaled[0] + mm_nt(g_key, wk_ref[...])).astype(BF16)
    spread = mm(src_t[...], back[:, 0:C])
    pad_rows = jnp.zeros((PAD - NODE_DEV, C), F32)
    for d in range(N_GRAPH):
        p0[d] = jnp.concatenate([spread[d * NODE_DEV : (d + 1) * NODE_DEV], pad_rows], axis=0).astype(BF16)

    def p0_copy(d):
        to = lax.rem(graph + d, N_GRAPH)
        return remote(p0.at[to], in0.at[d], r0_send.at[d], r0_recv.at[d], (dp, to))

    @pl.loop(1, N_GRAPH)
    def _(d):
        p0_copy(d).start()

    reduce_start(CHUNKS - 1)

    q_node = mm(dst_t[...], q_high) + mm(dst_t[...], q_low)
    q_node = q_node.astype(BF16)
    wpart[0:C] = mm_tn(x_ref[:, 0:C], q_node[0:NODE_DEV]).astype(BF16)
    wpart[C : 2 * C] = mm_tn(ex0[...], g_key).astype(BF16)
    rad_t = rad_ref[...].T
    for degree in range(LEVELS):
        g_pre = (fold[degree] * a * slope[degree]).astype(BF16)
        wpart[(2 + degree) * C : (3 + degree) * C] = mm(rad_t, g_pre).astype(BF16)
    for degree in range(LEVELS):
        begin, end = degree * degree, (degree + 1) * (degree + 1)
        sums = fwd[begin:end].reshape((end - begin) * NODE_DEV, C).astype(BF16)
        stacked = jnp.concatenate([cot_ref[:, k * C : (k + 1) * C].astype(F32) for k in range(begin, end)], axis=0)
        wpart[(9 + degree) * C : (10 + degree) * C] = mm_tn(sums, stacked.astype(BF16)).astype(BF16)

    def w1_copy(d):
        to = lax.rem(graph + d, N_GRAPH)
        piece = wpart.at[pl.ds(pl.multiple_of(to * GRAD_PIECE, GRAD_PIECE), GRAD_PIECE)]
        return remote(piece, win1.at[d], w1_send.at[d], w1_recv.at[d], (dp, to))

    @pl.loop(1, N_GRAPH)
    def _(d):
        w1_copy(d).start()

    for j in range(CHUNKS - 3, CHUNKS):
        reduce_next(j)

    for degree in range(LEVELS):
        begin, end = degree * degree, (degree + 1) * (degree + 1)
        sums = fwd[begin:end].reshape((end - begin) * NODE_DEV, C).astype(BF16)
        mixed = mm(sums, wd_ref[degree])
        for k in range(begin, end):
            rows = mixed[(k - begin) * NODE_DEV : (k - begin + 1) * NODE_DEV]
            upd_ref[:, k * C : (k + 1) * C] = (x_ref[:, k * C : (k + 1) * C].astype(F32) + rows).astype(BF16)

    @pl.loop(1, N_GRAPH)
    def _(d):
        w1_copy(d).wait_recv()

    total = wpart[pl.ds(pl.multiple_of(graph * GRAD_PIECE, GRAD_PIECE), GRAD_PIECE), :].astype(F32)
    for d in range(1, N_GRAPH):
        total = total + win1[d].astype(F32)
    win2[dp] = total.astype(BF16)

    def w2_copy(d):
        return remote(
            win2.at[dp], win2.at[dp], w2_send.at[d], w2_recv.at[d], (lax.rem(dp + d, N_DP), graph)
        )

    @pl.loop(1, N_DP)
    def _(d):
        w2_copy(d).start()

    @pl.loop(1, N_GRAPH)
    def _(d):
        p0_copy(d).wait_recv()

    total = p0[graph, 0:NODE_DEV, :].astype(F32)
    for d in range(1, N_GRAPH):
        total = total + in0[d, 0:NODE_DEV, :].astype(F32)
    total = total + cot_ref[:, 0:C].astype(F32) + mm_nt(q_node, wq_ref[...])[0:NODE_DEV]
    gn_ref[:, 0:C] = total.astype(BF16)

    @pl.loop(1, N_DP)
    def _(d):
        w2_copy(d).wait_recv()

    total = win2[0].astype(F32)
    for d in range(1, N_DP):
        total = total + win2[d].astype(F32)
    my_piece = pl.ds(pl.multiple_of(graph * GRAD_PIECE, GRAD_PIECE), GRAD_PIECE)
    wall[my_piece, :] = total.astype(BF16)

    def w3_copy(d):
        return remote(
            wall.at[my_piece], wall.at[my_piece], w3_send.at[d], w3_recv.at[d],
            (dp, lax.rem(graph + d, N_GRAPH)),
        )

    @pl.loop(1, N_GRAPH)
    def _(d):
        w3_copy(d).start()

    for j in range(CHUNKS - 5, CHUNKS):
        reduce_end(j)

    for j in range(CHUNKS):
        last_copy(j).wait_recv()
    for t in range(HALF_PAIRS):
        own = last[t, pl.ds(pl.multiple_of(core * NODE_DEV, 8), NODE_DEV), :]
        sib = last_in[t]
        for half in range(2):
            k = 1 + 2 * (half * HALF_PAIRS + t)
            spread = jnp.where(core == half, own, sib)
            cols = slice(k * C, (k + 2) * C)
            gn_ref[:, cols] = (cot_ref[:, cols].astype(F32) + spread).astype(BF16)

    @pl.loop(1, N_GRAPH)
    def _(d):
        w3_copy(d).wait_recv()

    gw_ref[...] = wall[...].astype(F32)

    sib_copy.wait_send()

    @pl.loop(1, N_GRAPH)
    def _(d):
        x0_copy(d).wait_send()
        p0_copy(d).wait_send()
        w1_copy(d).wait_send()
        w3_copy(d).wait_send()

    @pl.loop(1, N_DP)
    def _(d):
        w2_copy(d).wait_send()

    @pl.loop(0, CHUNKS)
    def _(j):
        for copy in gather_first(j) + gather_second(j) + reduce_first(j) + reduce_second(j):
            copy().wait_send()
        to_sibling(j).wait_send()
        sum_sibling(j).wait_send()
        last_copy(j).wait_send()


def on_device(node_feat, radial, src_node, dst_node, w_query, w_key, w_radial, w_degree, cotangent):
    vmem = pl.BlockSpec(memory_space=pltpu.VMEM)
    dma = pltpu.SemaphoreType.DMA
    width = node_feat.shape[2]
    scratch = [
        pltpu.VMEM((2, HALF_PAIRS, PAD, 2 * C), BF16),
        pltpu.VMEM((HALF_PAIRS, PAD, 2 * C), BF16),
        pltpu.VMEM((2, HALF_PAIRS, NODES, 2 * C), BF16),
        pltpu.VMEM((N_GRAPH, PAD, C), BF16),
        pltpu.VMEM((NODES, C), BF16),
        pltpu.VMEM((EDGE_DEV, NODES), BF16),
        pltpu.VMEM((NODES, EDGE_DEV), BF16),
        pltpu.VMEM((EDGE_DEV, PAD), BF16),
        pltpu.VMEM((PAD, EDGE_DEV), BF16),
        pltpu.VMEM((2 * HALF_PAIRS, PAD, 2 * C), BF16),
        pltpu.VMEM((PAD, C), BF16),
        pltpu.VMEM((LEVELS, EDGE_DEV, C), F32),
        pltpu.VMEM((LEVELS, EDGE_DEV, C), F32),
        pltpu.VMEM((LEVELS, EDGE_DEV, C), F32),
        pltpu.VMEM((LEVELS, EDGE_DEV, C), F32),
        pltpu.VMEM((LEVELS * LEVELS, NODE_DEV, C), F32),
        pltpu.VMEM((EDGE_DEV, 2 * C), BF16),
        pltpu.VMEM((EDGE_DEV, 2 * C), BF16),
        pltpu.VMEM((2, HALF_PAIRS, NODES, 2 * C), BF16),
        pltpu.VMEM((HALF_PAIRS, NODES, 2 * C), BF16),
        pltpu.VMEM((3, HALF_PAIRS, CHIP_ROWS, 2 * C), BF16),
        pltpu.VMEM((4, HALF_PAIRS, CHIP_ROWS, 2 * C), BF16),
        pltpu.VMEM((HALF_PAIRS, CHIP_ROWS, 2 * C), F32),
        pltpu.VMEM((HALF_PAIRS, NODE_DEV, 2 * C), F32),
        pltpu.VMEM((N_GRAPH, PAD, C), BF16),
        pltpu.VMEM((N_GRAPH, PAD, C), BF16),
        pltpu.VMEM((GRAD_ROWS, C), BF16),
        pltpu.VMEM((N_GRAPH, GRAD_PIECE, C), BF16),
        pltpu.VMEM((N_DP, GRAD_PIECE, C), BF16),
        pltpu.VMEM((GRAD_ROWS, C), BF16),
        pltpu.VMEM((EDGE_DEV, C), F32),
        pltpu.VMEM((EDGE_DEV, C), F32),
        pltpu.VMEM((EDGE_DEV, C), F32),
        pltpu.VMEM((EDGE_DEV, C), BF16),
        pltpu.VMEM((EDGE_DEV, C), F32),
        dma((2,)),
        dma((N_GRAPH,)),
        dma((N_GRAPH,)),
        dma((CHUNKS, 8)),
        dma((CHUNKS, 8)),
        dma((CHUNKS, 9)),
        dma((CHUNKS, 9)),
        dma((N_GRAPH,)),
        dma((N_GRAPH,)),
        dma((N_GRAPH,)),
        dma((N_GRAPH,)),
        dma((N_DP,)),
        dma((N_DP,)),
        dma((N_GRAPH,)),
        dma((N_GRAPH,)),
    ]
    updated, grad_node, grads = pl.pallas_call(
        kernel,
        out_shape=(
            jax.ShapeDtypeStruct((NODE_DEV, width), BF16),
            jax.ShapeDtypeStruct((NODE_DEV, width), BF16),
            jax.ShapeDtypeStruct((GRAD_ROWS, C), F32),
        ),
        in_specs=[vmem] * 9,
        out_specs=(vmem, vmem, vmem),
        scratch_shapes=scratch,
        compiler_params=pltpu.CompilerParams(
            collective_id=0, has_side_effects=True, vmem_limit_bytes=60 << 20
        ),
    )(node_feat[0], radial[0], src_node, dst_node, w_query, w_key, w_radial, w_degree, cotangent[0])
    grad_query = grads[0:C]
    grad_key = grads[C : 2 * C]
    grad_radial = jnp.concatenate([grads[(2 + d) * C : (3 + d) * C] for d in range(LEVELS)], axis=1)
    grad_degree = grads[9 * C :].reshape(LEVELS, C, C)
    return (updated[None], grad_node[None], grad_query, grad_key, grad_radial, grad_degree)


def solution(mesh):
    return jax.shard_map(
        on_device,
        mesh=mesh,
        in_specs=(
            P("dp", "graph", None),
            P("dp", "graph", None),
            P("dp", "graph"),
            P("dp", "graph"),
            P(),
            P(),
            P(),
            P(),
            P("dp", "graph", None),
        ),
        out_specs=(P("dp", "graph", None), P("dp", "graph", None), P(), P(), P(), P()),
        check_vma=False,
    )
```

time: 556 us -> 99.9 us (0.18)
  waiting for transfers between devices: 222 us -> 0 us
  local copies, waits for them, and re-layouts: 181 us -> 10.4 us
  matrix products: 108 us -> 0 us
  Pallas kernels: 0 us -> 88.3 us
  other arithmetic: 27.1 us -> 0 us
  between operations: 14.6 us -> 0.65 us
    psum x1 -> x0, waiting for transfers between devices: 139 us -> none  [on_device(): lax.psum((grad_query_local, grad_key_local, grad_radial_local, grad_degre...]
    dot_general x35 -> x0, matrix products: 108 us -> none  [the longest x1 29.8 us: on_device(): jnp.dot(dst_half, upstream_sum, preferred_element_type=jnp.float32)]
    mul x6 -> x0, local copies, waits for them, and re-layouts: 88.6 us -> none  [the longest x2 39 us: on_device(): grad_attn = jnp.sum(edge_grad * again3 * gate_full, axis=1)]
    pallas_call x0 -> x1, Pallas kernels: none -> 88.3 us  [on_device(): pl.pallas_call(kernel, out_shape=(jax.ShapeDtypeStruct((NODE_DEV, width),...]
    unnamed x4 -> x0, waiting for transfers between devices: 82.7 us -> none
    gather x5 -> x0, local copies, waits for them, and re-layouts: 49.3 us -> none  [the longest x3 47.6 us: on_device(): jax.nn.silu(pre_gate).reshape(edge_count, levels, channels)[:, table, :]]
    slice x19 -> x1, local copies, waits for them, and re-layouts: 17.3 us -> 2 us  [on_device(): grad_degree = grads[9 * C:].reshape(LEVELS, C, C)]
    mul x3 -> x0, other arithmetic: 15 us -> none  [the longest x1 14.9 us: on_device(): edge_grad * again3 * attn_again[:, None, :]]
  transfers between devices with their start and end apart: 3 -> 0, of which waited for: 2 -> 0; matrix products, arithmetic and copies ran while one was open for 15% -> 0% of each run, Pallas kernels for 0% -> 0%
where the time goes in v1:
time: 99.9 us; the launch traced here: 99.4 us
  Pallas kernels  88.3 us (88%)
  local copies, waits for them, and re-layouts  10.4 us (10%)
    pallas_call x1, Pallas kernels, on_device(): pl.pallas_call(kernel, out_shape=(jax.ShapeDtypeStruct((NODE_DEV, width),...  88.3 us
    unnamed x14, local copies, waits for them, and re-layouts  6.86 us
    slice x1, local copies, waits for them, and re-layouts, on_device(): grad_degree = grads[9 * C:].reshape(LEVELS, C, C)  2 us

profile of v1, /device:TPU:1, one launch (start us, length us, event | category | flops | bytes accessed | tf_op | source)
XLA Modules:
  0.0 99.4 jit_solution(4132293442412839698)
XLA Ops:
  0.6 88.3 %shard_map.136 = (bf16[24,6272]{1,0:T(8,128)(2,1)}, bf16[24,6272]{1,0:T(8,128)(2,1)}, f32[2048,128]{1,0:T(8,128)}) custom-call(bf16[24,6272]{1,0:T(8,128)(2,1)} %bitcast.9, bf16[768,128]{1,0:T(8,128)(2,1)} %bitcast.11, s32[1,768]{1,0:T(1,128)} %src_ref.1, s32[1,768]{1,0:T(1,128)} %dst_ref.1, bf16[128,128]{1,0:T(8,128)(2,1)} %wq_ref.1, ...), custom_call_target="tpu_custom_call" | custom-call | tf_op jit(solution)/shard_map/pallas_call | solution.py:582
  88.9 0.8 slice_dynamic-update-slice_fusion.6
  89.8 0.8 slice_dynamic-update-slice_fusion.5
  90.6 0.8 slice_dynamic-update-slice_fusion.4
  91.5 0.8 slice_dynamic-update-slice_fusion.3
  92.3 0.8 slice_dynamic-update-slice_fusion.2
  93.2 0.8 slice_dynamic-update-slice_fusion.1
  94.0 1.6 %slice_dynamic-update-slice_fusion = (f32[128,896]{1,0:T(8,128)S(1)}, f32[128,128]{1,0:T(8,128)}, f32[128,128]{1,0:T(8,128)}) fusion(f32[128,896]{1,0:T(8,128)S(1)} %slice_dynamic-update-slice_fusion.1, f32[2048,128]{1,0:T(8,128)} %get-tuple-element.11), kind=kLoop, calls=%fused_computation | loop fusion | bytes 393216 | tf_op jit(solution)/shard_map/concatenate | solution.py:598
  95.6 0.0 copy-start.2
  95.6 0.0 copy-start.1
  95.6 2.0 %slice.39 = f32[896,128]{1,0:T(8,128)} slice(f32[2048,128]{1,0:T(8,128)} %get-tuple-element.11), slice={[1152:2048], [0:128]} | slice | bytes 917504 | tf_op jit(solution)/shard_map/slice | solution.py:599
  97.6 0.0 copy-done.2
  97.6 0.0 copy-done.1
  97.6 0.0 copy-start
  97.6 0.7 copy.23
  98.3 0.4 copy-done
  98.7 0.7 copy.24
Async XLA Ops:
  95.6 2.0 %copy-start.2 = (f32[128,896]{1,0:T(8,128)}, f32[128,896]{1,0:T(8,128)S(1)}, u32[]{:S(2)}) copy-start(f32[128,896]{1,0:T(8,128)S(1)} %get-tuple-element.25) | copy-start | bytes 1376260
  95.6 2.0 %copy-start.1 = (bf16[24,6272]{1,0:T(8,128)(2,1)S(1)}, bf16[24,6272]{1,0:T(8,128)(2,1)}, u32[]{:S(2)}) copy-start(bf16[24,6272]{1,0:T(8,128)(2,1)} %get-tuple-element.9) | copy-start | bytes 903172
  97.6 1.1 %copy-start = (bf16[24,6272]{1,0:T(8,128)(2,1)S(1)}, bf16[24,6272]{1,0:T(8,128)(2,1)}, u32[]{:S(2)}) copy-start(bf16[24,6272]{1,0:T(8,128)(2,1)} %get-tuple-element.10) | copy-start | bytes 903172

commit v2 on v1

--- a/solution.py
+++ b/solution.py
@@ -22,8 +22,13 @@
 CHUNK = 2
 CHUNKS = HALF_PAIRS // CHUNK
 ROW_BLOCK = 256
-GRAD_ROWS = 2048
-GRAD_PIECE = GRAD_ROWS // N_GRAPH
+AHEAD = 2
+EARLY = 6
+EARLY_PIECE = 2 * EARLY * C // N_DP
+EARLY_PAD = 256
+EARLY_SUB = EARLY_PAD // N_GRAPH
+LATE_ROWS = 4 * C
+LATE_PIECE = LATE_ROWS // N_GRAPH
 MESH = pl.DeviceIdType.MESH
 F32 = jnp.float32
 BF16 = jnp.bfloat16
@@ -62,14 +67,15 @@
 
 def kernel(
     x_ref, rad_ref, src_ref, dst_ref, wq_ref, wk_ref, wr_ref, wd_ref, cot_ref,
-    upd_ref, gn_ref, gw_ref,
+    upd_ref, gn_ref, gq_ref, gk_ref, gr_ref, gd_ref,
     xs, sibx, xall, x0all, x0, src_hot, src_t, dst_hot, dst_t,
     gs, g0, gate, slope, scaled, fold, fwd, msg, back,
     part, from_sib, in_part, in_total, last, last_in, p0, in0,
-    wpart, win1, win2, wall,
+    wpart, win1, win2, wall, epart, ein1, esum, ein2, efull, eall,
     qe, key, att, ex0, gm0,
     sib_sems, x0_send, x0_recv, ag_send, ag_recv, rs_send, rs_recv,
     r0_send, r0_recv, w1_send, w1_recv, w2_send, w2_recv, w3_send, w3_recv,
+    e1_send, e1_recv, e2_send, e2_recv, e3_send, e3_recv, e4_send, e4_recv,
 ):
     dp = lax.axis_index("dp")
     graph = lax.axis_index("graph")
@@ -111,85 +117,10 @@
         )
 
     for pair in range(2 * HALF_PAIRS):
-        xs[pair // HALF_PAIRS, pair % HALF_PAIRS, 0:NODE_DEV, :] = x_ref[:, (1 + 2 * pair) * C : (3 + 2 * pair) * C]
-        xs[pair // HALF_PAIRS, pair % HALF_PAIRS, NODE_DEV:PAD, :] = jnp.zeros((PAD - NODE_DEV, 2 * C), BF16)
+        xs[pair % 2, pair // 2, 0:NODE_DEV, :] = x_ref[:, (1 + 2 * pair) * C : (3 + 2 * pair) * C]
+        xs[pair % 2, pair // 2, NODE_DEV:PAD, :] = jnp.zeros((PAD - NODE_DEV, 2 * C), BF16)
     x0all[graph, 0:NODE_DEV, :] = x_ref[:, 0:C]
     x0all[graph, NODE_DEV:PAD, :] = jnp.zeros((PAD - NODE_DEV, C), BF16)
-
-    pl.semaphore_wait(barrier, N_GRAPH - 1 + N_DP - 1)
-
-    sib_copy = remote(xs.at[other], sibx, sib_sems.at[0], sib_sems.at[1], sibling)
-    sib_copy.start()
-
-    def x0_copy(d):
-        return remote(
-            x0all.at[graph], x0all.at[graph], x0_send.at[d], x0_recv.at[d],
-            (dp, lax.rem(graph + d, N_GRAPH)),
-        )
-
-    @pl.loop(1, N_GRAPH)
-    def _(d):
-        x0_copy(d).start()
-
-    sib_copy.wait_recv()
-    mine = xs[core, :, 0:NODE_DEV, :].astype(F32)
-    theirs = sibx[:, 0:NODE_DEV, :].astype(F32)
-    first = jnp.where(core == 0, mine, theirs)
-    second = jnp.where(core == 0, theirs, mine)
-    xall[core, :, rows_of(chip), :] = jnp.concatenate([first, second], axis=1).astype(BF16)
-
-    def block(j, which):
-        return xall.at[core, pl.ds(j * CHUNK, CHUNK), rows_of(which), :]
-
-    def gather_copy(j, kind, which, device):
-        return lambda: remote(
-            block(j, which), block(j, which), ag_send.at[j, kind], ag_recv.at[j, kind], device
-        )
-
-    def gather_first(j):
-        return [
-            gather_copy(j, X_OWN, chip, at(1, 0)),
-            gather_copy(j, UP_OWN, chip, at(0, 1)),
-            gather_copy(j, DOWN_OWN, chip, at(0, 3)),
-            gather_copy(j, FAR_OWN, chip, at(0, 2)),
-        ]
-
-    def gather_second(j):
-        return [
-            gather_copy(j, UP_RELAY, chip_at(1, 0), at(0, 1)),
-            gather_copy(j, DOWN_RELAY, chip_at(1, 0), at(0, 3)),
-            gather_copy(j, X_RELAY, chip_at(0, 2), at(1, 0)),
-        ]
-
-    def to_sibling(j):
-        ref = xall.at[core, pl.ds(j * CHUNK, CHUNK)]
-        return remote(ref, ref, ag_send.at[j, TO_SIB], ag_recv.at[j, TO_SIB], sibling)
-
-    def got_block(j, kind, which):
-        gather_copy(j, kind, which, at(0, 1))().wait_recv()
-
-    @pl.loop(0, CHUNKS)
-    def _(j):
-        for copy in gather_first(j):
-            copy().start()
-
-    def relay(j):
-        got_block(j, X_OWN, chip_at(1, 0))
-        got_block(j, FAR_OWN, chip_at(0, 2))
-        for copy in gather_second(j):
-            copy().start()
-
-    def forward(j):
-        got_block(j, UP_OWN, chip_at(0, 3))
-        got_block(j, DOWN_OWN, chip_at(0, 1))
-        got_block(j, UP_RELAY, chip_at(1, 3))
-        got_block(j, DOWN_RELAY, chip_at(1, 1))
-        got_block(j, X_RELAY, chip_at(1, 2))
-        to_sibling(j).start()
-
-    def from_sibling(j):
-        ref = xall.at[other, pl.ds(j * CHUNK, CHUNK)]
-        remote(ref, ref, ag_send.at[j, TO_SIB], ag_recv.at[j, TO_SIB], sibling).wait_recv()
 
     src_row = src_ref[...].astype(F32)
     dst_row = (dst_ref[...] - graph * NODE_DEV).astype(F32)
@@ -206,6 +137,86 @@
         gate[degree] = pre * sigma
         slope[degree] = sigma * (1.0 + pre * (1.0 - sigma))
         fold[degree] = jnp.zeros((EDGE_DEV, C), F32)
+
+    pl.semaphore_wait(barrier, N_GRAPH - 1 + N_DP - 1)
+
+    sib_copy = remote(xs.at[other], sibx, sib_sems.at[0], sib_sems.at[1], sibling)
+    sib_copy.start()
+
+    def x0_copy(d):
+        return remote(
+            x0all.at[graph], x0all.at[graph], x0_send.at[d], x0_recv.at[d],
+            (dp, lax.rem(graph + d, N_GRAPH)),
+        )
+
+    @pl.loop(1, N_GRAPH)
+    def _(d):
+        x0_copy(d).start()
+
+    sib_copy.wait_recv()
+    mine = xs[core, :, 0:NODE_DEV, :].astype(F32)
+    theirs = sibx[:, 0:NODE_DEV, :].astype(F32)
+    first = jnp.where(core == 0, mine, theirs)
+    second = jnp.where(core == 0, theirs, mine)
+    xall[core, :, rows_of(chip), :] = jnp.concatenate([first, second], axis=1).astype(BF16)
+
+    def block(j, which):
+        return xall.at[core, pl.ds(j * CHUNK, CHUNK), rows_of(which), :]
+
+    def gather_copy(j, kind, which, device):
+        return lambda: remote(
+            block(j, which), block(j, which), ag_send.at[j, kind], ag_recv.at[j, kind], device
+        )
+
+    def gather_first(j):
+        return [
+            gather_copy(j, X_OWN, chip, at(1, 0)),
+            gather_copy(j, UP_OWN, chip, at(0, 1)),
+            gather_copy(j, DOWN_OWN, chip, at(0, 3)),
+            gather_copy(j, FAR_OWN, chip, at(0, 2)),
+        ]
+
+    def gather_second(j):
+        return [
+            gather_copy(j, UP_RELAY, chip_at(1, 0), at(0, 1)),
+            gather_copy(j, DOWN_RELAY, chip_at(1, 0), at(0, 3)),
+            gather_copy(j, X_RELAY, chip_at(0, 2), at(1, 0)),
+        ]
+
+    def to_sibling(j):
+        ref = xall.at[core, pl.ds(j * CHUNK, CHUNK)]
+        return remote(ref, ref, ag_send.at[j, TO_SIB], ag_recv.at[j, TO_SIB], sibling)
+
+    def got_block(j, kind, which):
+        gather_copy(j, kind, which, at(0, 1))().wait_recv()
+
+    @pl.loop(0, AHEAD)
+    def _(j):
+        for copy in gather_first(j):
+            copy().start()
+
+    def relay(j):
+        got_block(j, X_OWN, chip_at(1, 0))
+        got_block(j, FAR_OWN, chip_at(0, 2))
+        for copy in gather_second(j):
+            copy().start()
+
+        @pl.when(j + AHEAD < CHUNKS)
+        def _():
+            for copy in gather_first(j + AHEAD):
+                copy().start()
+
+    def forward(j):
+        got_block(j, UP_OWN, chip_at(0, 3))
+        got_block(j, DOWN_OWN, chip_at(0, 1))
+        got_block(j, UP_RELAY, chip_at(1, 3))
+        got_block(j, DOWN_RELAY, chip_at(1, 1))
+        got_block(j, X_RELAY, chip_at(1, 2))
+        to_sibling(j).start()
+
+    def from_sibling(j):
+        ref = xall.at[other, pl.ds(j * CHUNK, CHUNK)]
+        remote(ref, ref, ag_send.at[j, TO_SIB], ag_recv.at[j, TO_SIB], sibling).wait_recv()
 
     zeros = jnp.zeros((PAD - NODE_DEV, C), F32)
     for degree in range(LEVELS):
@@ -253,7 +264,7 @@
     fwd[0] = mm(dst_t[...], (ex0_float * scaled[0]).astype(BF16))[0:NODE_DEV]
 
     def edges(half, t):
-        pair = half * HALF_PAIRS + t
+        pair = 2 * t + half
         k = 1 + 2 * pair
         left, right = degree_of(k), degree_of(k + 1)
         nodes = xall[half, t]
@@ -343,6 +354,94 @@
             last[t] = total
         last_copy(j).start()
 
+    def degree_grad(degree):
+        begin, end = degree * degree, (degree + 1) * (degree + 1)
+        sums = fwd[begin:end].reshape((end - begin) * NODE_DEV, C).astype(BF16)
+        stacked = jnp.concatenate([cot_ref[:, k * C : (k + 1) * C].astype(F32) for k in range(begin, end)], axis=0)
+        return mm_tn(sums, stacked.astype(BF16)).astype(BF16)
+
+    def radial_grad(degree):
+        g_pre = (fold[degree] * att[...] * slope[degree]).astype(BF16)
+        return mm_tn(rad_ref[...], g_pre).astype(BF16)
+
+    def dp_peer(d):
+        return lax.rem(dp + d, N_DP)
+
+    def graph_peer(d):
+        return lax.rem(graph + d, N_GRAPH)
+
+    def early_rows(which):
+        return pl.ds(pl.multiple_of(which * EARLY_PIECE, 16), EARLY_PIECE)
+
+    def e1_copy(d):
+        to = dp_peer(d)
+        return remote(epart.at[early_rows(to)], ein1.at[d], e1_send.at[d], e1_recv.at[d], (to, graph))
+
+    def sub_rows(which):
+        return pl.ds(pl.multiple_of(which * EARLY_SUB, EARLY_SUB), EARLY_SUB)
+
+    def e2_copy(d):
+        to = graph_peer(d)
+        return remote(esum.at[sub_rows(to)], ein2.at[d], e2_send.at[d], e2_recv.at[d], (dp, to))
+
+    def e3_copy(d):
+        mine = efull.at[sub_rows(graph)]
+        return remote(mine, mine, e3_send.at[d], e3_recv.at[d], (dp, graph_peer(d)))
+
+    def e4_copy(d):
+        mine = eall.at[early_rows(dp)]
+        return remote(mine, mine, e4_send.at[d], e4_recv.at[d], (dp_peer(d), graph))
+
+    def early_start():
+        for degree in range(EARLY):
+            epart[degree * C : (degree + 1) * C] = radial_grad(degree)
+            epart[(EARLY + degree) * C : (EARLY + degree + 1) * C] = degree_grad(degree)
+
+        @pl.loop(1, N_DP)
+        def _(d):
+            e1_copy(d).start()
+
+    def early_second():
+        @pl.loop(1, N_DP)
+        def _(d):
+            e1_copy(d).wait_recv()
+
+        total = epart[early_rows(dp), :].astype(F32)
+        for d in range(1, N_DP):
+            total = total + ein1[d].astype(F32)
+        esum[0:EARLY_PIECE] = total.astype(BF16)
+        esum[EARLY_PIECE:EARLY_PAD] = jnp.zeros((EARLY_PAD - EARLY_PIECE, C), BF16)
+
+        @pl.loop(1, N_GRAPH)
+        def _(d):
+            e2_copy(d).start()
+
+    def early_third():
+        @pl.loop(1, N_GRAPH)
+        def _(d):
+            e2_copy(d).wait_recv()
+
+        total = esum[sub_rows(graph), :].astype(F32)
+        for d in range(1, N_GRAPH):
+            total = total + ein2[d].astype(F32)
+
+        efull[sub_rows(graph), :] = total.astype(BF16)
+
+        @pl.loop(1, N_GRAPH)
+        def _(d):
+            e3_copy(d).start()
+
+    def early_fourth():
+        @pl.loop(1, N_GRAPH)
+        def _(d):
+            e3_copy(d).wait_recv()
+
+        eall[early_rows(dp), :] = efull[0:EARLY_PIECE]
+
+        @pl.loop(1, N_DP)
+        def _(d):
+            e4_copy(d).start()
+
     @pl.loop(0, CHUNKS)
     def _(s):
         @pl.when(s + 2 < CHUNKS)
@@ -352,6 +451,10 @@
         @pl.when(s + 1 < CHUNKS)
         def _():
             forward(s + 1)
+
+        @pl.when(s == CHUNKS - 1)
+        def _():
+            early_start()
 
         from_sibling(s)
 
@@ -397,32 +500,26 @@
     def _(d):
         p0_copy(d).start()
 
-    reduce_start(CHUNKS - 1)
-
-    q_node = mm(dst_t[...], q_high) + mm(dst_t[...], q_low)
-    q_node = q_node.astype(BF16)
+    q_node = (mm(dst_t[...], q_high) + mm(dst_t[...], q_low)).astype(BF16)
     wpart[0:C] = mm_tn(x_ref[:, 0:C], q_node[0:NODE_DEV]).astype(BF16)
     wpart[C : 2 * C] = mm_tn(ex0[...], g_key).astype(BF16)
-    rad_t = rad_ref[...].T
-    for degree in range(LEVELS):
-        g_pre = (fold[degree] * a * slope[degree]).astype(BF16)
-        wpart[(2 + degree) * C : (3 + degree) * C] = mm(rad_t, g_pre).astype(BF16)
-    for degree in range(LEVELS):
-        begin, end = degree * degree, (degree + 1) * (degree + 1)
-        sums = fwd[begin:end].reshape((end - begin) * NODE_DEV, C).astype(BF16)
-        stacked = jnp.concatenate([cot_ref[:, k * C : (k + 1) * C].astype(F32) for k in range(begin, end)], axis=0)
-        wpart[(9 + degree) * C : (10 + degree) * C] = mm_tn(sums, stacked.astype(BF16)).astype(BF16)
+    wpart[2 * C : 3 * C] = radial_grad(EARLY)
+    wpart[3 * C : 4 * C] = degree_grad(EARLY)
+
+    def late_rows(which):
+        return pl.ds(pl.multiple_of(which * LATE_PIECE, LATE_PIECE), LATE_PIECE)
 
     def w1_copy(d):
-        to = lax.rem(graph + d, N_GRAPH)
-        piece = wpart.at[pl.ds(pl.multiple_of(to * GRAD_PIECE, GRAD_PIECE), GRAD_PIECE)]
-        return remote(piece, win1.at[d], w1_send.at[d], w1_recv.at[d], (dp, to))
+        to = graph_peer(d)
+        return remote(wpart.at[late_rows(to)], win1.at[d], w1_send.at[d], w1_recv.at[d], (dp, to))
 
     @pl.loop(1, N_GRAPH)
     def _(d):
         w1_copy(d).start()
 
-    for j in range(CHUNKS - 3, CHUNKS):
+    reduce_start(CHUNKS - 1)
+    early_second()
+    for j in range(CHUNKS - 3, CHUNKS - 1):
         reduce_next(j)
 
     for degree in range(LEVELS):
@@ -433,23 +530,26 @@
             rows = mixed[(k - begin) * NODE_DEV : (k - begin + 1) * NODE_DEV]
             upd_ref[:, k * C : (k + 1) * C] = (x_ref[:, k * C : (k + 1) * C].astype(F32) + rows).astype(BF16)
 
+    early_third()
+
     @pl.loop(1, N_GRAPH)
     def _(d):
         w1_copy(d).wait_recv()
 
-    total = wpart[pl.ds(pl.multiple_of(graph * GRAD_PIECE, GRAD_PIECE), GRAD_PIECE), :].astype(F32)
+    total = wpart[late_rows(graph), :].astype(F32)
     for d in range(1, N_GRAPH):
         total = total + win1[d].astype(F32)
     win2[dp] = total.astype(BF16)
 
     def w2_copy(d):
-        return remote(
-            win2.at[dp], win2.at[dp], w2_send.at[d], w2_recv.at[d], (lax.rem(dp + d, N_DP), graph)
-        )
+        return remote(win2.at[dp], win2.at[dp], w2_send.at[d], w2_recv.at[d], (dp_peer(d), graph))
 
     @pl.loop(1, N_DP)
     def _(d):
         w2_copy(d).start()
+
+    reduce_next(CHUNKS - 1)
+    early_fourth()
 
     @pl.loop(1, N_GRAPH)
     def _(d):
@@ -468,14 +568,11 @@
     total = win2[0].astype(F32)
     for d in range(1, N_DP):
         total = total + win2[d].astype(F32)
-    my_piece = pl.ds(pl.multiple_of(graph * GRAD_PIECE, GRAD_PIECE), GRAD_PIECE)
-    wall[my_piece, :] = total.astype(BF16)
+    wall[late_rows(graph), :] = total.astype(BF16)
 
     def w3_copy(d):
-        return remote(
-            wall.at[my_piece], wall.at[my_piece], w3_send.at[d], w3_recv.at[d],
-            (dp, lax.rem(graph + d, N_GRAPH)),
-        )
+        mine = wall.at[late_rows(graph)]
+        return remote(mine, mine, w3_send.at[d], w3_recv.at[d], (dp, graph_peer(d)))
 
     @pl.loop(1, N_GRAPH)
     def _(d):
@@ -490,16 +587,27 @@
         own = last[t, pl.ds(pl.multiple_of(core * NODE_DEV, 8), NODE_DEV), :]
         sib = last_in[t]
         for half in range(2):
-            k = 1 + 2 * (half * HALF_PAIRS + t)
+            k = 1 + 2 * (2 * t + half)
             spread = jnp.where(core == half, own, sib)
             cols = slice(k * C, (k + 2) * C)
             gn_ref[:, cols] = (cot_ref[:, cols].astype(F32) + spread).astype(BF16)
 
+    @pl.loop(1, N_DP)
+    def _(d):
+        e4_copy(d).wait_recv()
+
+    for degree in range(EARLY):
+        gr_ref[:, degree * C : (degree + 1) * C] = eall[degree * C : (degree + 1) * C].astype(F32)
+        gd_ref[degree] = eall[(EARLY + degree) * C : (EARLY + degree + 1) * C].astype(F32)
+
     @pl.loop(1, N_GRAPH)
     def _(d):
         w3_copy(d).wait_recv()
 
-    gw_ref[...] = wall[...].astype(F32)
+    gq_ref[...] = wall[0:C].astype(F32)
+    gk_ref[...] = wall[C : 2 * C].astype(F32)
+    gr_ref[:, EARLY * C :] = wall[2 * C : 3 * C].astype(F32)
+    gd_ref[EARLY] = wall[3 * C : 4 * C].astype(F32)
 
     sib_copy.wait_send()
 
@@ -509,10 +617,14 @@
         p0_copy(d).wait_send()
         w1_copy(d).wait_send()
         w3_copy(d).wait_send()
+        e2_copy(d).wait_send()
+        e3_copy(d).wait_send()
 
     @pl.loop(1, N_DP)
     def _(d):
         w2_copy(d).wait_send()
+        e1_copy(d).wait_send()
+        e4_copy(d).wait_send()
 
     @pl.loop(0, CHUNKS)
     def _(j):
@@ -554,10 +666,16 @@
         pltpu.VMEM((HALF_PAIRS, NODE_DEV, 2 * C), F32),
         pltpu.VMEM((N_GRAPH, PAD, C), BF16),
         pltpu.VMEM((N_GRAPH, PAD, C), BF16),
-        pltpu.VMEM((GRAD_ROWS, C), BF16),
-        pltpu.VMEM((N_GRAPH, GRAD_PIECE, C), BF16),
-        pltpu.VMEM((N_DP, GRAD_PIECE, C), BF16),
-        pltpu.VMEM((GRAD_ROWS, C), BF16),
+        pltpu.VMEM((LATE_ROWS, C), BF16),
+        pltpu.VMEM((N_GRAPH, LATE_PIECE, C), BF16),
+        pltpu.VMEM((N_DP, LATE_PIECE, C), BF16),
+        pltpu.VMEM((LATE_ROWS, C), BF16),
+        pltpu.VMEM((2 * EARLY * C, C), BF16),
+        pltpu.VMEM((N_DP, EARLY_PIECE, C), BF16),
+        pltpu.VMEM((EARLY_PAD, C), BF16),
+        pltpu.VMEM((N_GRAPH, EARLY_SUB, C), BF16),
+        pltpu.VMEM((EARLY_PAD, C), BF16),
+        pltpu.VMEM((2 * EARLY * C, C), BF16),
         pltpu.VMEM((EDGE_DEV, C), F32),
         pltpu.VMEM((EDGE_DEV, C), F32),
         pltpu.VMEM((EDGE_DEV, C), F32),
@@ -578,25 +696,32 @@
         dma((N_DP,)),
         dma((N_GRAPH,)),
         dma((N_GRAPH,)),
+        dma((N_DP,)),
+        dma((N_DP,)),
+        dma((N_GRAPH,)),
+        dma((N_GRAPH,)),
+        dma((N_GRAPH,)),
+        dma((N_GRAPH,)),
+        dma((N_DP,)),
+        dma((N_DP,)),
     ]
-    updated, grad_node, grads = pl.pallas_call(
+    updated, grad_node, grad_query, grad_key, grad_radial, grad_degree = pl.pallas_call(
         kernel,
         out_shape=(
             jax.ShapeDtypeStruct((NODE_DEV, width), BF16),
             jax.ShapeDtypeStruct((NODE_DEV, width), BF16),
-            jax.ShapeDtypeStruct((GRAD_ROWS, C), F32),
+            jax.ShapeDtypeStruct((C, C), F32),
+            jax.ShapeDtypeStruct((C, C), F32),
+            jax.ShapeDtypeStruct((C, LEVELS * C), F32),
+            jax.ShapeDtypeStruct((LEVELS, C, C), F32),
         ),
         in_specs=[vmem] * 9,
-        out_specs=(vmem, vmem, vmem),
+        out_specs=(vmem,) * 6,
         scratch_shapes=scratch,
         compiler_params=pltpu.CompilerParams(
             collective_id=0, has_side_effects=True, vmem_limit_bytes=60 << 20
         ),
     )(node_feat[0], radial[0], src_node, dst_node, w_query, w_key, w_radial, w_degree, cotangent[0])
-    grad_query = grads[0:C]
-    grad_key = grads[C : 2 * C]
-    grad_radial = jnp.concatenate([grads[(2 + d) * C : (3 + d) * C] for d in range(LEVELS)], axis=1)
-    grad_degree = grads[9 * C :].reshape(LEVELS, C, C)
     return (updated[None], grad_node[None], grad_query, grad_key, grad_radial, grad_degree)
 
 

time: 99.9 us -> 84.8 us (0.85)
  Pallas kernels: 88.3 us -> 77.9 us
  local copies, waits for them, and re-layouts: 10.4 us -> 6.05 us
    pallas_call x1, Pallas kernels: 88.3 us -> 77.9 us  [on_device(): pl.pallas_call(kernel, out_shape=(jax.ShapeDtypeStruct((NODE_DEV, width),...]
    slice x1 -> x0, local copies, waits for them, and re-layouts: 2 us -> none  [on_device(): grad_degree = grads[9 * C:].reshape(LEVELS, C, C)]
    concatenate x1 -> x0, local copies, waits for them, and re-layouts: 1.56 us -> none  [on_device(): jnp.concatenate([grads[(2 + d) * C:(3 + d) * C] for d in range(LEVELS)],...]
    unnamed x14 -> x16, local copies, waits for them, and re-layouts: 6.86 us -> 6.05 us
where the time goes in v2:
time: 84.8 us; the launch traced here: 84.6 us
  Pallas kernels  77.9 us (92%)
  local copies, waits for them, and re-layouts  6.05 us (7%)
    pallas_call x1, Pallas kernels, on_device(): pl.pallas_call(kernel, out_shape=(jax.ShapeDtypeStruct((NODE_DEV, width),...  77.9 us
    unnamed x16, local copies, waits for them, and re-layouts  6.05 us

profile of v2, /device:TPU:1, one launch (start us, length us, event | category | flops | bytes accessed | tf_op | source)
XLA Modules:
  0.0 84.6 jit_solution(17801071571104621130)
XLA Ops:
  0.6 77.9 %shard_map.136 = (bf16[24,6272]{1,0:T(8,128)(2,1)}, bf16[24,6272]{1,0:T(8,128)(2,1)}, f32[128,128]{1,0:T(8,128)}, f32[128,128]{1,0:T(8,128)}, f32[128,896]{1,0:T(8,128)}, /*index=5*/f32[7,128,128]{2,1,0:T(8,128)}) custom-call(bf16[24,6272]{1,0:T(8,128)(2,1)} %bitcast.7, bf16[768,128]{1,0:T(8,128)(2,1)} %bitcast.9, s32[1,768]{1,0:T(1,128)} %src_ref.1, ...), custom_call_target="tpu_custom_call" | custom-call | tf_op jit(solution)/shard_map/pallas_call | solution.py:708
  78.5 0.0 copy-start.2
  78.5 1.7 %copy.21 = bf16[1,24,6272]{2,1,0:T(8,128)(2,1)} copy(bf16[1,24,6272]{2,1,0:T(8,128)(2,1)} %bitcast.6) | data formatting | bytes 602112
  80.3 0.0 copy-done.2
  80.3 0.0 copy-start.4
  80.3 0.0 copy-start.1
  80.3 0.7 copy.22
  81.0 0.1 copy-done.4
  81.1 0.0 copy-start.3
  81.1 0.6 copy.23
  81.8 0.2 copy-done.3
  82.0 0.6 copy.24
  82.6 0.0 copy-done.1
  82.6 0.0 copy-start
  82.6 0.8 copy.25
  83.4 0.4 copy-done
  83.8 0.8 copy.26
Async XLA Ops:
  78.5 1.8 %copy-start.2 = (bf16[24,6272]{1,0:T(8,128)(2,1)S(1)}, bf16[24,6272]{1,0:T(8,128)(2,1)}, u32[]{:S(2)}) copy-start(bf16[24,6272]{1,0:T(8,128)(2,1)} %get-tuple-element.13) | copy-start | bytes 903172
  80.3 0.9 %copy-start.4 = (f32[128,128]{1,0:T(8,128)S(1)}, f32[128,128]{1,0:T(8,128)}, u32[]{:S(2)}) copy-start(f32[128,128]{1,0:T(8,128)} %get-tuple-element.26) | copy-start | bytes 196612
  80.3 2.4 %copy-start.1 = (f32[128,896]{1,0:T(8,128)S(1)}, f32[128,896]{1,0:T(8,128)}, u32[]{:S(2)}) copy-start(f32[128,896]{1,0:T(8,128)} %get-tuple-element.28) | copy-start | bytes 1376260
  81.1 0.9 %copy-start.3 = (f32[128,128]{1,0:T(8,128)S(1)}, f32[128,128]{1,0:T(8,128)}, u32[]{:S(2)}) copy-start(f32[128,128]{1,0:T(8,128)} %get-tuple-element.27) | copy-start | bytes 196612
  82.6 1.2 %copy-start = (f32[7,128,128]{2,1,0:T(8,128)S(1)}, f32[7,128,128]{2,1,0:T(8,128)}, u32[]{:S(2)}) copy-start(f32[7,128,128]{2,1,0:T(8,128)} %get-tuple-element.29) | copy-start | bytes 1376260

commit v3 on v1

--- a/solution.py
+++ b/solution.py
@@ -21,15 +21,25 @@
 HALF_PAIRS = 12
 CHUNK = 2
 CHUNKS = HALF_PAIRS // CHUNK
-ROW_BLOCK = 256
-GRAD_ROWS = 2048
-GRAD_PIECE = GRAD_ROWS // N_GRAPH
+ROW_BLOCK = 128
+AHEAD = 2
+NEXT_LAG = 2
+END_LAG = 4
+EARLY = 5
+EARLY_HALF = EARLY * C
+EARLY_PIECE = EARLY_HALF // N_DP
+EARLY_PAD = 128
+N_CHIP = N_GRAPH // 2
+EARLY_SUB = EARLY_PAD // N_CHIP
+LATE_DEGREES = LEVELS - EARLY
+LATE_ROWS = (2 + 2 * LATE_DEGREES) * C
+LATE_PIECE = LATE_ROWS // N_GRAPH
 MESH = pl.DeviceIdType.MESH
 F32 = jnp.float32
 BF16 = jnp.bfloat16
 
-X_OWN, UP_OWN, DOWN_OWN, FAR_OWN, UP_RELAY, DOWN_RELAY, X_RELAY, TO_SIB = range(8)
-SUM_SIB, PART_UP, PART_DOWN, PART_X, OWN_UP, OWN_DOWN, TOTAL_X, TOTAL_FAR, LAST_SIB = range(9)
+FIRST, REST, SIB = range(3)
+PARTS, TOTALS, LAST = range(1, 4)
 
 
 def mm(a, b):
@@ -62,14 +72,15 @@
 
 def kernel(
     x_ref, rad_ref, src_ref, dst_ref, wq_ref, wk_ref, wr_ref, wd_ref, cot_ref,
-    upd_ref, gn_ref, gw_ref,
+    upd_ref, gn_ref, ge_ref, gl_ref,
     xs, sibx, xall, x0all, x0, src_hot, src_t, dst_hot, dst_t,
     gs, g0, gate, slope, scaled, fold, fwd, msg, back,
     part, from_sib, in_part, in_total, last, last_in, p0, in0,
-    wpart, win1, win2, wall,
-    qe, key, att, ex0, gm0,
+    wpart, win1, win2, wall, epart, esib, e1_in, esum, e2_in, efull, eall,
+    qe, key, att, ex0, gm0, rad_t,
     sib_sems, x0_send, x0_recv, ag_send, ag_recv, rs_send, rs_recv,
     r0_send, r0_recv, w1_send, w1_recv, w2_send, w2_recv, w3_send, w3_recv,
+    e_send, e_recv,
 ):
     dp = lax.axis_index("dp")
     graph = lax.axis_index("graph")
@@ -111,8 +122,8 @@
         )
 
     for pair in range(2 * HALF_PAIRS):
-        xs[pair // HALF_PAIRS, pair % HALF_PAIRS, 0:NODE_DEV, :] = x_ref[:, (1 + 2 * pair) * C : (3 + 2 * pair) * C]
-        xs[pair // HALF_PAIRS, pair % HALF_PAIRS, NODE_DEV:PAD, :] = jnp.zeros((PAD - NODE_DEV, 2 * C), BF16)
+        xs[pair % 2, pair // 2, 0:NODE_DEV, :] = x_ref[:, (1 + 2 * pair) * C : (3 + 2 * pair) * C]
+        xs[pair % 2, pair // 2, NODE_DEV:PAD, :] = jnp.zeros((PAD - NODE_DEV, 2 * C), BF16)
     x0all[graph, 0:NODE_DEV, :] = x_ref[:, 0:C]
     x0all[graph, NODE_DEV:PAD, :] = jnp.zeros((PAD - NODE_DEV, C), BF16)
 
@@ -123,7 +134,7 @@
 
     def x0_copy(d):
         return remote(
-            x0all.at[graph], x0all.at[graph], x0_send.at[d], x0_recv.at[d],
+            x0all.at[graph], x0all.at[graph], x0_send.at[0], x0_recv.at[0],
             (dp, lax.rem(graph + d, N_GRAPH)),
         )
 
@@ -141,55 +152,54 @@
     def block(j, which):
         return xall.at[core, pl.ds(j * CHUNK, CHUNK), rows_of(which), :]
 
-    def gather_copy(j, kind, which, device):
-        return lambda: remote(
-            block(j, which), block(j, which), ag_send.at[j, kind], ag_recv.at[j, kind], device
-        )
+    def gather_copy(j, group, which, device):
+        return lambda: remote(block(j, which), block(j, which), ag_send.at[0], ag_recv.at[j, group], device)
 
     def gather_first(j):
         return [
-            gather_copy(j, X_OWN, chip, at(1, 0)),
-            gather_copy(j, UP_OWN, chip, at(0, 1)),
-            gather_copy(j, DOWN_OWN, chip, at(0, 3)),
-            gather_copy(j, FAR_OWN, chip, at(0, 2)),
+            gather_copy(j, FIRST, chip, at(1, 0)),
+            gather_copy(j, REST, chip, at(0, 1)),
+            gather_copy(j, REST, chip, at(0, 3)),
+            gather_copy(j, FIRST, chip, at(0, 2)),
         ]
 
     def gather_second(j):
         return [
-            gather_copy(j, UP_RELAY, chip_at(1, 0), at(0, 1)),
-            gather_copy(j, DOWN_RELAY, chip_at(1, 0), at(0, 3)),
-            gather_copy(j, X_RELAY, chip_at(0, 2), at(1, 0)),
+            gather_copy(j, REST, chip_at(1, 0), at(0, 1)),
+            gather_copy(j, REST, chip_at(1, 0), at(0, 3)),
+            gather_copy(j, REST, chip_at(0, 2), at(1, 0)),
         ]
 
     def to_sibling(j):
         ref = xall.at[core, pl.ds(j * CHUNK, CHUNK)]
-        return remote(ref, ref, ag_send.at[j, TO_SIB], ag_recv.at[j, TO_SIB], sibling)
-
-    def got_block(j, kind, which):
-        gather_copy(j, kind, which, at(0, 1))().wait_recv()
-
-    @pl.loop(0, CHUNKS)
+        return remote(ref, ref, ag_send.at[1], ag_recv.at[j, SIB], sibling)
+
+    def got_blocks(j, group, count):
+        ref = xall.at[core, pl.ds(j * CHUNK, CHUNK), pl.ds(0, count * CHIP_ROWS), :]
+        remote(ref, ref, ag_send.at[0], ag_recv.at[j, group], sibling).wait_recv()
+
+    @pl.loop(0, AHEAD)
     def _(j):
         for copy in gather_first(j):
             copy().start()
 
     def relay(j):
-        got_block(j, X_OWN, chip_at(1, 0))
-        got_block(j, FAR_OWN, chip_at(0, 2))
+        got_blocks(j, FIRST, 2)
         for copy in gather_second(j):
             copy().start()
 
+        @pl.when(j + AHEAD < CHUNKS)
+        def _():
+            for copy in gather_first(j + AHEAD):
+                copy().start()
+
     def forward(j):
-        got_block(j, UP_OWN, chip_at(0, 3))
-        got_block(j, DOWN_OWN, chip_at(0, 1))
-        got_block(j, UP_RELAY, chip_at(1, 3))
-        got_block(j, DOWN_RELAY, chip_at(1, 1))
-        got_block(j, X_RELAY, chip_at(1, 2))
+        got_blocks(j, REST, 5)
         to_sibling(j).start()
 
     def from_sibling(j):
         ref = xall.at[other, pl.ds(j * CHUNK, CHUNK)]
-        remote(ref, ref, ag_send.at[j, TO_SIB], ag_recv.at[j, TO_SIB], sibling).wait_recv()
+        remote(ref, ref, ag_send.at[1], ag_recv.at[j, SIB], sibling).wait_recv()
 
     src_row = src_ref[...].astype(F32)
     dst_row = (dst_ref[...] - graph * NODE_DEV).astype(F32)
@@ -200,6 +210,7 @@
     src_hot[...] = (lax.broadcasted_iota(jnp.int32, (EDGE_DEV, NODES), 1).astype(F32) == src_col).astype(F32).astype(BF16)
     dst_hot[...] = (lax.broadcasted_iota(jnp.int32, (EDGE_DEV, PAD), 1).astype(F32) == dst_col).astype(F32).astype(BF16)
 
+    rad_t[...] = rad_ref[...].T
     for degree in range(LEVELS):
         pre = mm(rad_ref[...], wr_ref[:, degree * C : (degree + 1) * C])
         sigma = jax.nn.sigmoid(pre)
@@ -207,6 +218,7 @@
         slope[degree] = sigma * (1.0 + pre * (1.0 - sigma))
         fold[degree] = jnp.zeros((EDGE_DEV, C), F32)
 
+    relay(0)
     zeros = jnp.zeros((PAD - NODE_DEV, C), F32)
     for degree in range(LEVELS):
         begin, end = degree * degree, (degree + 1) * (degree + 1)
@@ -235,12 +247,10 @@
         high, low = two_parts(a)
         return mm(high, same_head) + mm(low, same_head)
 
-    @pl.loop(1, N_GRAPH)
-    def _(d):
-        x0_copy(d).wait_recv()
+    remote(x0all.at[pl.ds(1, N_GRAPH - 1)], x0all.at[pl.ds(1, N_GRAPH - 1)], x0_send.at[0], x0_recv.at[0], sibling).wait_recv()
 
     x0[...] = jnp.concatenate([x0all[d, 0:NODE_DEV, :].astype(F32) for d in range(N_GRAPH)], axis=0).astype(BF16)
-    relay(0)
+    relay(1)
     ex0[...] = mm(src_hot[...], x0[...]).astype(BF16)
     key[...] = mm(ex0[...], wk_ref[...])
     att[...] = jax.nn.sigmoid(head_sum(qe[...] * key[...]) * scale)
@@ -248,12 +258,11 @@
         scaled[degree] = gate[degree] * att[...]
     ex0_float = ex0[...].astype(F32)
     fold[0] = ex0_float * gm0[...]
-    relay(1)
     forward(0)
     fwd[0] = mm(dst_t[...], (ex0_float * scaled[0]).astype(BF16))[0:NODE_DEV]
 
     def edges(half, t):
-        pair = half * HALF_PAIRS + t
+        pair = 2 * t + half
         k = 1 + 2 * pair
         left, right = degree_of(k), degree_of(k + 1)
         nodes = xall[half, t]
@@ -276,38 +285,38 @@
     def sum_sibling(j):
         return remote(
             part.at[other, pl.ds(j * CHUNK, CHUNK)], from_sib.at[pl.ds(j * CHUNK, CHUNK)],
-            rs_send.at[j, SUM_SIB], rs_recv.at[j, SUM_SIB], sibling,
+            rs_send.at[0], rs_recv.at[j, 0], sibling,
         )
 
     def part_block(j, which):
         return part.at[core, pl.ds(j * CHUNK, CHUNK), rows_of(which), :]
 
-    def reduce_copy(j, kind, which, landing, slot, device):
+    def reduce_copy(j, group, which, landing, slot, device):
         return lambda: remote(
             part_block(j, which), landing.at[slot, pl.ds(j * CHUNK, CHUNK)],
-            rs_send.at[j, kind], rs_recv.at[j, kind], device,
+            rs_send.at[1], rs_recv.at[j, group], device,
         )
 
     def reduce_first(j):
         return [
-            reduce_copy(j, PART_UP, chip_at(1, 1), in_part, 0, at(0, 1)),
-            reduce_copy(j, PART_DOWN, chip_at(1, 3), in_part, 1, at(0, 3)),
-            reduce_copy(j, PART_X, chip_at(1, 2), in_part, 2, at(1, 0)),
-            reduce_copy(j, OWN_UP, chip_at(0, 1), in_total, 0, at(0, 1)),
-            reduce_copy(j, OWN_DOWN, chip_at(0, 3), in_total, 1, at(0, 3)),
+            reduce_copy(j, PARTS, chip_at(1, 1), in_part, 0, at(0, 1)),
+            reduce_copy(j, PARTS, chip_at(1, 3), in_part, 1, at(0, 3)),
+            reduce_copy(j, PARTS, chip_at(1, 2), in_part, 2, at(1, 0)),
+            reduce_copy(j, TOTALS, chip_at(0, 1), in_total, 0, at(0, 1)),
+            reduce_copy(j, TOTALS, chip_at(0, 3), in_total, 1, at(0, 3)),
         ]
 
     def reduce_second(j):
         return [
-            reduce_copy(j, TOTAL_X, chip_at(1, 0), in_total, 2, at(1, 0)),
-            reduce_copy(j, TOTAL_FAR, chip_at(0, 2), in_total, 3, at(0, 2)),
+            reduce_copy(j, TOTALS, chip_at(1, 0), in_total, 2, at(1, 0)),
+            reduce_copy(j, TOTALS, chip_at(0, 2), in_total, 3, at(0, 2)),
         ]
 
     def last_copy(j):
         return remote(
             last.at[pl.ds(j * CHUNK, CHUNK), pl.ds(pl.multiple_of(other * NODE_DEV, 8), NODE_DEV), :],
             last_in.at[pl.ds(j * CHUNK, CHUNK)],
-            rs_send.at[j, LAST_SIB], rs_recv.at[j, LAST_SIB], sibling,
+            rs_send.at[2], rs_recv.at[j, LAST], sibling,
         )
 
     def reduce_start(j):
@@ -319,8 +328,8 @@
             copy().start()
 
     def reduce_next(j):
-        for copy in reduce_first(j)[:3]:
-            copy().wait_recv()
+        ref = in_part.at[:, pl.ds(j * CHUNK, CHUNK)]
+        remote(ref, ref, rs_send.at[1], rs_recv.at[j, PARTS], sibling).wait_recv()
         for i in range(CHUNK):
             t = j * CHUNK + i
             rows = rows_of(chip_at(1, 0))
@@ -333,8 +342,8 @@
             copy().start()
 
     def reduce_end(j):
-        for copy in reduce_first(j)[3:] + reduce_second(j):
-            copy().wait_recv()
+        ref = in_total.at[:, pl.ds(j * CHUNK, CHUNK)]
+        remote(ref, ref, rs_send.at[1], rs_recv.at[j, TOTALS], sibling).wait_recv()
         for i in range(CHUNK):
             t = j * CHUNK + i
             total = part[core, t, rows_of(chip), :].astype(F32)
@@ -343,6 +352,108 @@
             last[t] = total
         last_copy(j).start()
 
+    def degree_grad(degree):
+        begin, end = degree * degree, (degree + 1) * (degree + 1)
+        sums = fwd[begin:end].reshape((end - begin) * NODE_DEV, C).astype(BF16)
+        stacked = jnp.concatenate([cot_ref[:, k * C : (k + 1) * C].astype(F32) for k in range(begin, end)], axis=0)
+        return mm_tn(sums, stacked.astype(BF16)).astype(BF16)
+
+    def radial_grad(degree):
+        g_pre = (fold[degree] * att[...] * slope[degree]).astype(BF16)
+        return mm(rad_t[...], g_pre).astype(BF16)
+
+    def dp_peer(d):
+        return lax.rem(dp + d, N_DP)
+
+    def graph_peer(d):
+        return lax.rem(graph + d, N_GRAPH)
+
+    def early_rows(half, which=0, count=1):
+        return pl.ds(pl.multiple_of(half * EARLY_HALF + which * EARLY_PIECE, 16), count * EARLY_PIECE)
+
+    def sub_rows(which):
+        return pl.ds(pl.multiple_of(which * EARLY_SUB, 16), EARLY_SUB)
+
+    def chip_peer(d):
+        return lax.rem(chip + d, N_CHIP)
+
+    def e0_copy():
+        return remote(epart.at[early_rows(other, 0, N_DP)], esib, e_send.at[0], e_recv.at[0], sibling)
+
+    def e1_copy(d):
+        to = dp_peer(d)
+        return remote(epart.at[early_rows(core, to)], e1_in.at[d], e_send.at[1], e_recv.at[1], (to, graph))
+
+    def e2_copy(d):
+        to = chip_peer(d)
+        return remote(esum.at[sub_rows(to)], e2_in.at[d], e_send.at[2], e_recv.at[2], (dp, to * 2 + core))
+
+    def e3_copy(d):
+        mine = efull.at[sub_rows(chip)]
+        return remote(mine, mine, e_send.at[3], e_recv.at[3], (dp, chip_peer(d) * 2 + core))
+
+    def e4_copy(d):
+        mine = eall.at[early_rows(core, dp)]
+        return remote(mine, mine, e_send.at[4], e_recv.at[4], (dp_peer(d), graph))
+
+    def e5_copy():
+        mine = eall.at[early_rows(core, 0, N_DP)]
+        return remote(mine, mine, e_send.at[5], e_recv.at[5], sibling)
+
+    def early_first():
+        for degree in range(EARLY):
+            epart[2 * degree * C : (2 * degree + 1) * C] = radial_grad(degree)
+            epart[(2 * degree + 1) * C : (2 * degree + 2) * C] = degree_grad(degree)
+        e0_copy().start()
+
+    def early_second():
+        e0_copy().wait_recv()
+        rows = early_rows(core, 0, N_DP)
+        epart[rows, :] = (epart[rows, :].astype(F32) + esib[...].astype(F32)).astype(BF16)
+
+        @pl.loop(1, N_DP)
+        def _(d):
+            e1_copy(d).start()
+
+    def early_third():
+        ref = e1_in.at[pl.ds(1, N_DP - 1)]
+        remote(ref, ref, e_send.at[1], e_recv.at[1], sibling).wait_recv()
+        total = epart[early_rows(core, dp), :].astype(F32)
+        for d in range(1, N_DP):
+            total = total + e1_in[d].astype(F32)
+        esum[0:EARLY_PIECE] = total.astype(BF16)
+        esum[EARLY_PIECE:EARLY_PAD] = jnp.zeros((EARLY_PAD - EARLY_PIECE, C), BF16)
+
+        @pl.loop(1, N_CHIP)
+        def _(d):
+            e2_copy(d).start()
+
+    def early_fourth():
+        ref = e2_in.at[pl.ds(1, N_CHIP - 1)]
+        remote(ref, ref, e_send.at[2], e_recv.at[2], sibling).wait_recv()
+        total = esum[sub_rows(chip), :].astype(F32)
+        for d in range(1, N_CHIP):
+            total = total + e2_in[d].astype(F32)
+        efull[sub_rows(chip), :] = total.astype(BF16)
+
+        @pl.loop(1, N_CHIP)
+        def _(d):
+            e3_copy(d).start()
+
+    def early_fifth():
+        ref = e2_in.at[pl.ds(1, N_CHIP - 1)]
+        remote(ref, ref, e_send.at[3], e_recv.at[3], sibling).wait_recv()
+        eall[early_rows(core, dp), :] = efull[0:EARLY_PIECE]
+
+        @pl.loop(1, N_DP)
+        def _(d):
+            e4_copy(d).start()
+
+    def early_sixth():
+        ref = e1_in.at[pl.ds(1, N_DP - 1)]
+        remote(ref, ref, e_send.at[4], e_recv.at[4], sibling).wait_recv()
+        e5_copy().start()
+
     @pl.loop(0, CHUNKS)
     def _(s):
         @pl.when(s + 2 < CHUNKS)
@@ -353,6 +464,10 @@
         def _():
             forward(s + 1)
 
+        @pl.when(s == CHUNKS - 3)
+        def _():
+            early_first()
+
         from_sibling(s)
 
         @pl.loop(0, 2 * CHUNK)
@@ -368,13 +483,21 @@
         def _():
             reduce_start(s - 1)
 
-        @pl.when(s >= 3)
+        @pl.when(s >= NEXT_LAG)
         def _():
-            reduce_next(s - 3)
-
-        @pl.when(s >= 5)
+            reduce_next(s - NEXT_LAG)
+
+        @pl.when(s >= END_LAG)
         def _():
-            reduce_end(s - 5)
+            reduce_end(s - END_LAG)
+
+        @pl.when(s == CHUNKS - 3)
+        def _():
+            early_second()
+
+    reduce_start(CHUNKS - 1)
+
+    early_third()
 
     a = att[...]
     g_att = gate[0] * fold[0]
@@ -383,6 +506,24 @@
     g_logit = head_sum(g_att) * a * (1.0 - a) * scale
     g_key = (g_logit * qe[...]).astype(BF16)
     q_high, q_low = two_parts(g_logit * key[...])
+    q_node = (mm(dst_t[...], q_high) + mm(dst_t[...], q_low)).astype(BF16)
+    wpart[0:C] = mm_tn(x_ref[:, 0:C], q_node[0:NODE_DEV]).astype(BF16)
+    wpart[C : 2 * C] = mm_tn(ex0[...], g_key).astype(BF16)
+    for i in range(LATE_DEGREES):
+        wpart[(2 + 2 * i) * C : (3 + 2 * i) * C] = radial_grad(EARLY + i)
+        wpart[(3 + 2 * i) * C : (4 + 2 * i) * C] = degree_grad(EARLY + i)
+
+    def late_rows(which):
+        return pl.ds(pl.multiple_of(which * LATE_PIECE, 16), LATE_PIECE)
+
+    def w1_copy(d):
+        to = graph_peer(d)
+        return remote(wpart.at[late_rows(to)], win1.at[d], w1_send.at[0], w1_recv.at[0], (dp, to))
+
+    @pl.loop(1, N_GRAPH)
+    def _(d):
+        w1_copy(d).start()
+
     back[:, 0:C] = (gm0[...] * scaled[0] + mm_nt(g_key, wk_ref[...])).astype(BF16)
     spread = mm(src_t[...], back[:, 0:C])
     pad_rows = jnp.zeros((PAD - NODE_DEV, C), F32)
@@ -391,38 +532,14 @@
 
     def p0_copy(d):
         to = lax.rem(graph + d, N_GRAPH)
-        return remote(p0.at[to], in0.at[d], r0_send.at[d], r0_recv.at[d], (dp, to))
+        return remote(p0.at[to], in0.at[d], r0_send.at[0], r0_recv.at[0], (dp, to))
 
     @pl.loop(1, N_GRAPH)
     def _(d):
         p0_copy(d).start()
 
-    reduce_start(CHUNKS - 1)
-
-    q_node = mm(dst_t[...], q_high) + mm(dst_t[...], q_low)
-    q_node = q_node.astype(BF16)
-    wpart[0:C] = mm_tn(x_ref[:, 0:C], q_node[0:NODE_DEV]).astype(BF16)
-    wpart[C : 2 * C] = mm_tn(ex0[...], g_key).astype(BF16)
-    rad_t = rad_ref[...].T
-    for degree in range(LEVELS):
-        g_pre = (fold[degree] * a * slope[degree]).astype(BF16)
-        wpart[(2 + degree) * C : (3 + degree) * C] = mm(rad_t, g_pre).astype(BF16)
-    for degree in range(LEVELS):
-        begin, end = degree * degree, (degree + 1) * (degree + 1)
-        sums = fwd[begin:end].reshape((end - begin) * NODE_DEV, C).astype(BF16)
-        stacked = jnp.concatenate([cot_ref[:, k * C : (k + 1) * C].astype(F32) for k in range(begin, end)], axis=0)
-        wpart[(9 + degree) * C : (10 + degree) * C] = mm_tn(sums, stacked.astype(BF16)).astype(BF16)
-
-    def w1_copy(d):
-        to = lax.rem(graph + d, N_GRAPH)
-        piece = wpart.at[pl.ds(pl.multiple_of(to * GRAD_PIECE, GRAD_PIECE), GRAD_PIECE)]
-        return remote(piece, win1.at[d], w1_send.at[d], w1_recv.at[d], (dp, to))
-
-    @pl.loop(1, N_GRAPH)
-    def _(d):
-        w1_copy(d).start()
-
-    for j in range(CHUNKS - 3, CHUNKS):
+    early_fourth()
+    for j in range(CHUNKS - NEXT_LAG, CHUNKS):
         reduce_next(j)
 
     for degree in range(LEVELS):
@@ -433,56 +550,49 @@
             rows = mixed[(k - begin) * NODE_DEV : (k - begin + 1) * NODE_DEV]
             upd_ref[:, k * C : (k + 1) * C] = (x_ref[:, k * C : (k + 1) * C].astype(F32) + rows).astype(BF16)
 
-    @pl.loop(1, N_GRAPH)
-    def _(d):
-        w1_copy(d).wait_recv()
-
-    total = wpart[pl.ds(pl.multiple_of(graph * GRAD_PIECE, GRAD_PIECE), GRAD_PIECE), :].astype(F32)
+    remote(win1.at[pl.ds(1, N_GRAPH - 1)], win1.at[pl.ds(1, N_GRAPH - 1)], w1_send.at[0], w1_recv.at[0], sibling).wait_recv()
+
+    total = wpart[late_rows(graph), :].astype(F32)
     for d in range(1, N_GRAPH):
         total = total + win1[d].astype(F32)
     win2[dp] = total.astype(BF16)
 
     def w2_copy(d):
-        return remote(
-            win2.at[dp], win2.at[dp], w2_send.at[d], w2_recv.at[d], (lax.rem(dp + d, N_DP), graph)
-        )
+        return remote(win2.at[dp], win2.at[dp], w2_send.at[0], w2_recv.at[0], (dp_peer(d), graph))
 
     @pl.loop(1, N_DP)
     def _(d):
         w2_copy(d).start()
 
+    early_fifth()
+    for j in range(CHUNKS - END_LAG, CHUNKS - 1):
+        reduce_end(j)
+
+    remote(win2.at[pl.ds(1, N_DP - 1)], win2.at[pl.ds(1, N_DP - 1)], w2_send.at[0], w2_recv.at[0], sibling).wait_recv()
+
+    total = win2[0].astype(F32)
+    for d in range(1, N_DP):
+        total = total + win2[d].astype(F32)
+    wall[late_rows(graph), :] = total.astype(BF16)
+
+    def w3_copy(d):
+        mine = wall.at[late_rows(graph)]
+        return remote(mine, mine, w3_send.at[0], w3_recv.at[0], (dp, graph_peer(d)))
+
     @pl.loop(1, N_GRAPH)
     def _(d):
-        p0_copy(d).wait_recv()
+        w3_copy(d).start()
+
+    early_sixth()
+    reduce_end(CHUNKS - 1)
+
+    remote(in0.at[pl.ds(1, N_GRAPH - 1)], in0.at[pl.ds(1, N_GRAPH - 1)], r0_send.at[0], r0_recv.at[0], sibling).wait_recv()
 
     total = p0[graph, 0:NODE_DEV, :].astype(F32)
     for d in range(1, N_GRAPH):
         total = total + in0[d, 0:NODE_DEV, :].astype(F32)
     total = total + cot_ref[:, 0:C].astype(F32) + mm_nt(q_node, wq_ref[...])[0:NODE_DEV]
     gn_ref[:, 0:C] = total.astype(BF16)
-
-    @pl.loop(1, N_DP)
-    def _(d):
-        w2_copy(d).wait_recv()
-
-    total = win2[0].astype(F32)
-    for d in range(1, N_DP):
-        total = total + win2[d].astype(F32)
-    my_piece = pl.ds(pl.multiple_of(graph * GRAD_PIECE, GRAD_PIECE), GRAD_PIECE)
-    wall[my_piece, :] = total.astype(BF16)
-
-    def w3_copy(d):
-        return remote(
-            wall.at[my_piece], wall.at[my_piece], w3_send.at[d], w3_recv.at[d],
-            (dp, lax.rem(graph + d, N_GRAPH)),
-        )
-
-    @pl.loop(1, N_GRAPH)
-    def _(d):
-        w3_copy(d).start()
-
-    for j in range(CHUNKS - 5, CHUNKS):
-        reduce_end(j)
 
     for j in range(CHUNKS):
         last_copy(j).wait_recv()
@@ -490,37 +600,49 @@
         own = last[t, pl.ds(pl.multiple_of(core * NODE_DEV, 8), NODE_DEV), :]
         sib = last_in[t]
         for half in range(2):
-            k = 1 + 2 * (half * HALF_PAIRS + t)
+            k = 1 + 2 * (2 * t + half)
             spread = jnp.where(core == half, own, sib)
             cols = slice(k * C, (k + 2) * C)
             gn_ref[:, cols] = (cot_ref[:, cols].astype(F32) + spread).astype(BF16)
 
-    @pl.loop(1, N_GRAPH)
-    def _(d):
-        w3_copy(d).wait_recv()
-
-    gw_ref[...] = wall[...].astype(F32)
+    e5_copy().wait_recv()
+    ge_ref[...] = eall[...]
+
+    remote(wall.at[pl.ds(0, (N_GRAPH - 1) * LATE_PIECE)], wall.at[pl.ds(0, (N_GRAPH - 1) * LATE_PIECE)], w3_send.at[0], w3_recv.at[0], sibling).wait_recv()
+
+    gl_ref[...] = wall[...]
 
     sib_copy.wait_send()
-
-    @pl.loop(1, N_GRAPH)
-    def _(d):
-        x0_copy(d).wait_send()
-        p0_copy(d).wait_send()
-        w1_copy(d).wait_send()
-        w3_copy(d).wait_send()
-
-    @pl.loop(1, N_DP)
-    def _(d):
-        w2_copy(d).wait_send()
-
-    @pl.loop(0, CHUNKS)
-    def _(j):
-        for copy in gather_first(j) + gather_second(j) + reduce_first(j) + reduce_second(j):
-            copy().wait_send()
-        to_sibling(j).wait_send()
-        sum_sibling(j).wait_send()
-        last_copy(j).wait_send()
+    remote(x0all.at[pl.ds(1, N_GRAPH - 1)], x0all.at[pl.ds(1, N_GRAPH - 1)], x0_send.at[0], x0_recv.at[0], sibling).wait_send()
+    remote(in0.at[pl.ds(1, N_GRAPH - 1)], in0.at[pl.ds(1, N_GRAPH - 1)], r0_send.at[0], r0_recv.at[0], sibling).wait_send()
+    remote(win1.at[pl.ds(1, N_GRAPH - 1)], win1.at[pl.ds(1, N_GRAPH - 1)], w1_send.at[0], w1_recv.at[0], sibling).wait_send()
+    remote(win2.at[pl.ds(1, N_DP - 1)], win2.at[pl.ds(1, N_DP - 1)], w2_send.at[0], w2_recv.at[0], sibling).wait_send()
+    remote(wall.at[pl.ds(0, (N_GRAPH - 1) * LATE_PIECE)], wall.at[pl.ds(0, (N_GRAPH - 1) * LATE_PIECE)], w3_send.at[0], w3_recv.at[0], sibling).wait_send()
+    remote(xall.at[0, :, pl.ds(0, 7 * CHIP_ROWS), :], xall.at[0, :, pl.ds(0, 7 * CHIP_ROWS), :], ag_send.at[0], e_recv.at[0], sibling).wait_send()
+    remote(xall.at[0], xall.at[0], ag_send.at[1], e_recv.at[0], sibling).wait_send()
+    remote(from_sib, from_sib, rs_send.at[0], e_recv.at[0], sibling).wait_send()
+    remote(xall.at[0, :, pl.ds(0, 7 * CHIP_ROWS), :], xall.at[0, :, pl.ds(0, 7 * CHIP_ROWS), :], rs_send.at[1], e_recv.at[0], sibling).wait_send()
+    remote(last_in, last_in, rs_send.at[2], e_recv.at[0], sibling).wait_send()
+    remote(e1_in.at[pl.ds(1, N_DP - 1)], e1_in.at[pl.ds(1, N_DP - 1)], e_send.at[1], e_recv.at[0], sibling).wait_send()
+    remote(e2_in.at[pl.ds(1, N_CHIP - 1)], e2_in.at[pl.ds(1, N_CHIP - 1)], e_send.at[2], e_recv.at[0], sibling).wait_send()
+    remote(e2_in.at[pl.ds(1, N_CHIP - 1)], e2_in.at[pl.ds(1, N_CHIP - 1)], e_send.at[3], e_recv.at[0], sibling).wait_send()
+    remote(e1_in.at[pl.ds(1, N_DP - 1)], e1_in.at[pl.ds(1, N_DP - 1)], e_send.at[4], e_recv.at[0], sibling).wait_send()
+    remote(esib, esib, e_send.at[0], e_recv.at[0], sibling).wait_send()
+    remote(esib, esib, e_send.at[5], e_recv.at[0], sibling).wait_send()
+
+
+def write_kernel(u_ref, n_ref, ge_ref, gl_ref, upd_ref, gn_ref, gq_ref, gk_ref, gr_ref, gd_ref):
+    upd_ref[...] = u_ref[...]
+    gn_ref[...] = n_ref[...]
+    for degree in range(EARLY):
+        gr_ref[:, degree * C : (degree + 1) * C] = ge_ref[2 * degree * C : (2 * degree + 1) * C].astype(F32)
+        gd_ref[degree] = ge_ref[(2 * degree + 1) * C : (2 * degree + 2) * C].astype(F32)
+    gq_ref[...] = gl_ref[0:C].astype(F32)
+    gk_ref[...] = gl_ref[C : 2 * C].astype(F32)
+    for i in range(LATE_DEGREES):
+        degree = EARLY + i
+        gr_ref[:, degree * C : (degree + 1) * C] = gl_ref[(2 + 2 * i) * C : (3 + 2 * i) * C].astype(F32)
+        gd_ref[degree] = gl_ref[(3 + 2 * i) * C : (4 + 2 * i) * C].astype(F32)
 
 
 def on_device(node_feat, radial, src_node, dst_node, w_query, w_key, w_radial, w_degree, cotangent):
@@ -554,49 +676,70 @@
         pltpu.VMEM((HALF_PAIRS, NODE_DEV, 2 * C), F32),
         pltpu.VMEM((N_GRAPH, PAD, C), BF16),
         pltpu.VMEM((N_GRAPH, PAD, C), BF16),
-        pltpu.VMEM((GRAD_ROWS, C), BF16),
-        pltpu.VMEM((N_GRAPH, GRAD_PIECE, C), BF16),
-        pltpu.VMEM((N_DP, GRAD_PIECE, C), BF16),
-        pltpu.VMEM((GRAD_ROWS, C), BF16),
+        pltpu.VMEM((LATE_ROWS, C), BF16),
+        pltpu.VMEM((N_GRAPH, LATE_PIECE, C), BF16),
+        pltpu.VMEM((N_DP, LATE_PIECE, C), BF16),
+        pltpu.VMEM((LATE_ROWS, C), BF16),
+        pltpu.VMEM((2 * EARLY_HALF, C), BF16),
+        pltpu.VMEM((EARLY_HALF, C), BF16),
+        pltpu.VMEM((N_DP, EARLY_PIECE, C), BF16),
+        pltpu.VMEM((EARLY_PAD, C), BF16),
+        pltpu.VMEM((N_CHIP, EARLY_SUB, C), BF16),
+        pltpu.VMEM((EARLY_PAD, C), BF16),
+        pltpu.VMEM((2 * EARLY_HALF, C), BF16),
         pltpu.VMEM((EDGE_DEV, C), F32),
         pltpu.VMEM((EDGE_DEV, C), F32),
         pltpu.VMEM((EDGE_DEV, C), F32),
         pltpu.VMEM((EDGE_DEV, C), BF16),
         pltpu.VMEM((EDGE_DEV, C), F32),
+        pltpu.VMEM((C, EDGE_DEV), BF16),
         dma((2,)),
-        dma((N_GRAPH,)),
-        dma((N_GRAPH,)),
-        dma((CHUNKS, 8)),
-        dma((CHUNKS, 8)),
-        dma((CHUNKS, 9)),
-        dma((CHUNKS, 9)),
-        dma((N_GRAPH,)),
-        dma((N_GRAPH,)),
-        dma((N_GRAPH,)),
-        dma((N_GRAPH,)),
-        dma((N_DP,)),
-        dma((N_DP,)),
-        dma((N_GRAPH,)),
-        dma((N_GRAPH,)),
+        dma((1,)),
+        dma((1,)),
+        dma((2,)),
+        dma((CHUNKS, 3)),
+        dma((3,)),
+        dma((CHUNKS, 4)),
+        dma((1,)),
+        dma((1,)),
+        dma((1,)),
+        dma((1,)),
+        dma((1,)),
+        dma((1,)),
+        dma((1,)),
+        dma((1,)),
+        dma((6,)),
+        dma((6,)),
     ]
-    updated, grad_node, grads = pl.pallas_call(
+    updated, grad_node, early, late = pl.pallas_call(
         kernel,
         out_shape=(
             jax.ShapeDtypeStruct((NODE_DEV, width), BF16),
             jax.ShapeDtypeStruct((NODE_DEV, width), BF16),
-            jax.ShapeDtypeStruct((GRAD_ROWS, C), F32),
+            jax.ShapeDtypeStruct((2 * EARLY * C, C), BF16),
+            jax.ShapeDtypeStruct((LATE_ROWS, C), BF16),
         ),
         in_specs=[vmem] * 9,
-        out_specs=(vmem, vmem, vmem),
+        out_specs=(vmem,) * 4,
         scratch_shapes=scratch,
         compiler_params=pltpu.CompilerParams(
             collective_id=0, has_side_effects=True, vmem_limit_bytes=60 << 20
         ),
     )(node_feat[0], radial[0], src_node, dst_node, w_query, w_key, w_radial, w_degree, cotangent[0])
-    grad_query = grads[0:C]
-    grad_key = grads[C : 2 * C]
-    grad_radial = jnp.concatenate([grads[(2 + d) * C : (3 + d) * C] for d in range(LEVELS)], axis=1)
-    grad_degree = grads[9 * C :].reshape(LEVELS, C, C)
+    updated, grad_node, grad_query, grad_key, grad_radial, grad_degree = pl.pallas_call(
+        write_kernel,
+        out_shape=(
+            jax.ShapeDtypeStruct((NODE_DEV, width), BF16),
+            jax.ShapeDtypeStruct((NODE_DEV, width), BF16),
+            jax.ShapeDtypeStruct((C, C), F32),
+            jax.ShapeDtypeStruct((C, C), F32),
+            jax.ShapeDtypeStruct((C, LEVELS * C), F32),
+            jax.ShapeDtypeStruct((LEVELS, C, C), F32),
+        ),
+        in_specs=[vmem] * 4,
+        out_specs=(vmem,) * 6,
+        compiler_params=pltpu.CompilerParams(vmem_limit_bytes=32 << 20),
+    )(updated, grad_node, early, late)
     return (updated[None], grad_node[None], grad_query, grad_key, grad_radial, grad_degree)
 
 

time: 99.9 us -> 76.9 us (0.77)
  Pallas kernels: 88.3 us -> 72.2 us
  local copies, waits for them, and re-layouts: 10.4 us -> 3.82 us
    pallas_call x1, Pallas kernels: 88.3 us -> 70.9 us  [on_device(): pl.pallas_call(kernel, out_shape=(jax.ShapeDtypeStruct((NODE_DEV, width),...]
    unnamed x14 -> x8, local copies, waits for them, and re-layouts: 6.86 us -> 3.82 us
    slice x1 -> x0, local copies, waits for them, and re-layouts: 2 us -> none  [on_device(): grad_degree = grads[9 * C:].reshape(LEVELS, C, C)]
    concatenate x1 -> x0, local copies, waits for them, and re-layouts: 1.56 us -> none  [on_device(): jnp.concatenate([grads[(2 + d) * C:(3 + d) * C] for d in range(LEVELS)],...]
    pallas_call x0 -> x1, Pallas kernels: none -> 1.25 us  [on_device(): pl.pallas_call(write_kernel, out_shape=(jax.ShapeDtypeStruct((NODE_DEV, w...]
where the time goes in v3:
time: 76.9 us; the launch traced here: 76.7 us
  Pallas kernels  72.2 us (94%)
  local copies, waits for them, and re-layouts  3.82 us (5%)
    pallas_call x1, Pallas kernels, on_device(): pl.pallas_call(kernel, out_shape=(jax.ShapeDtypeStruct((NODE_DEV, width),...  70.9 us
    unnamed x8, local copies, waits for them, and re-layouts  3.82 us

profile of v3, /device:TPU:1, one launch (start us, length us, event | category | flops | bytes accessed | tf_op | source)
XLA Modules:
  0.0 76.7 jit_solution(10722718236703620422)
XLA Ops:
  0.6 70.9 %shard_map.136 = (bf16[24,6272]{1,0:T(8,128)(2,1)}, bf16[24,6272]{1,0:T(8,128)(2,1)}, bf16[1280,128]{1,0:T(8,128)(2,1)}, bf16[768,128]{1,0:T(8,128)(2,1)}) custom-call(bf16[24,6272]{1,0:T(8,128)(2,1)} %bitcast.5, bf16[768,128]{1,0:T(8,128)(2,1)} %bitcast.7, s32[1,768]{1,0:T(1,128)} %src_ref.1, s32[1,768]{1,0:T(1,128)} %dst_ref.1, bf16[128,128]{1,0:T(8,128)(2,1)} %wq_ref.1, ...), custom_call_target="tpu_custom_call" | custom-call | tf_op jit(solution)/shard_map/pallas_call | solution.py:714
  71.6 0.0 copy-start
  71.6 1.0 %copy-done = bf16[1280,128]{1,0:T(8,128)(2,1)S(1)} copy-done((bf16[1280,128]{1,0:T(8,128)(2,1)S(1)}, bf16[1280,128]{1,0:T(8,128)(2,1)}, u32[]{:S(2)}) %copy-start) | copy-done | bytes 327704
  72.6 0.0 copy-start.1
  72.6 1.0 %copy-done.1 = bf16[24,6272]{1,0:T(8,128)(2,1)S(1)} copy-done((bf16[24,6272]{1,0:T(8,128)(2,1)S(1)}, bf16[24,6272]{1,0:T(8,128)(2,1)}, u32[]{:S(2)}) %copy-start.1) | copy-done | bytes 301080
  73.5 0.0 copy-start.2
  73.5 1.0 %copy-done.2 = bf16[24,6272]{1,0:T(8,128)(2,1)S(1)} copy-done((bf16[24,6272]{1,0:T(8,128)(2,1)S(1)}, bf16[24,6272]{1,0:T(8,128)(2,1)}, u32[]{:S(2)}) %copy-start.2) | copy-done | bytes 301080
  74.5 0.0 copy-start.3
  74.5 0.9 %copy-done.3 = bf16[768,128]{1,0:T(8,128)(2,1)S(1)} copy-done((bf16[768,128]{1,0:T(8,128)(2,1)S(1)}, bf16[768,128]{1,0:T(8,128)(2,1)}, u32[]{:S(2)}) %copy-start.3) | copy-done | bytes 196632
  75.4 1.2 %shard_map.137 = (bf16[24,6272]{1,0:T(8,128)(2,1)}, bf16[24,6272]{1,0:T(8,128)(2,1)}, f32[128,128]{1,0:T(8,128)}, f32[128,128]{1,0:T(8,128)}, f32[128,896]{1,0:T(8,128)}, /*index=5*/f32[7,128,128]{2,1,0:T(8,128)}) custom-call(bf16[24,6272]{1,0:T(8,128)(2,1)S(1)} %copy-done.1, bf16[24,6272]{1,0:T(8,128)(2,1)S(1)} %copy-done.2, bf16[1280,128]{1,0:T(8,128)(2,1)S(1)} %copy-done, ...), custom_call_target="tpu_custom_call" | custom-call | tf_op jit(solution)/shard_map/pallas_call | solution.py:729
Async XLA Ops:
  71.6 1.0 %copy-start = (bf16[1280,128]{1,0:T(8,128)(2,1)S(1)}, bf16[1280,128]{1,0:T(8,128)(2,1)}, u32[]{:S(2)}) copy-start(bf16[1280,128]{1,0:T(8,128)(2,1)} %get-tuple-element.18.ge_ref) | copy-start | bytes 983044
  72.6 1.0 %copy-start.1 = (bf16[24,6272]{1,0:T(8,128)(2,1)S(1)}, bf16[24,6272]{1,0:T(8,128)(2,1)}, u32[]{:S(2)}) copy-start(bf16[24,6272]{1,0:T(8,128)(2,1)} %get-tuple-element.16.u_ref) | copy-start | bytes 903172
  73.5 1.0 %copy-start.2 = (bf16[24,6272]{1,0:T(8,128)(2,1)S(1)}, bf16[24,6272]{1,0:T(8,128)(2,1)}, u32[]{:S(2)}) copy-start(bf16[24,6272]{1,0:T(8,128)(2,1)} %get-tuple-element.17.n_ref) | copy-start | bytes 903172
  74.5 0.9 %copy-start.3 = (bf16[768,128]{1,0:T(8,128)(2,1)S(1)}, bf16[768,128]{1,0:T(8,128)(2,1)}, u32[]{:S(2)}) copy-start(bf16[768,128]{1,0:T(8,128)(2,1)} %get-tuple-element.19.gl_ref) | copy-start | bytes 589828

commit v4 on v3

--- a/solution.py
+++ b/solution.py
@@ -23,6 +23,7 @@
 CHUNKS = HALF_PAIRS // CHUNK
 ROW_BLOCK = 128
 AHEAD = 2
+LEAD = 2
 NEXT_LAG = 2
 END_LAG = 4
 EARLY = 5
@@ -456,28 +457,27 @@
 
     @pl.loop(0, CHUNKS)
     def _(s):
-        @pl.when(s + 2 < CHUNKS)
+        @pl.when(s + LEAD < CHUNKS)
         def _():
-            relay(s + 2)
-
-        @pl.when(s + 1 < CHUNKS)
-        def _():
-            forward(s + 1)
+            relay(s + LEAD)
 
         @pl.when(s == CHUNKS - 3)
         def _():
             early_first()
 
-        from_sibling(s)
-
         @pl.loop(0, 2 * CHUNK)
         def _(i):
-            half = lax.rem(other + i // CHUNK, 2)
-            edges(half, s * CHUNK + lax.rem(i, CHUNK))
-
-            @pl.when(i == CHUNK - 1)
+            @pl.when(i == CHUNK)
             def _():
-                sum_sibling(s).start()
+                @pl.when(s + 1 < CHUNKS)
+                def _():
+                    forward(s + 1)
+
+                from_sibling(s)
+
+            edges(lax.rem(core + i // CHUNK, 2), s * CHUNK + lax.rem(i, CHUNK))
+
+        sum_sibling(s).start()
 
         @pl.when(s >= 1)
         def _():

time: 76.9 us -> 72.9 us (0.948)
  Pallas kernels: 72.2 us -> 68.1 us
    pallas_call x1, Pallas kernels: 70.9 us -> 66.9 us  [on_device(): pl.pallas_call(kernel, out_shape=(jax.ShapeDtypeStruct((NODE_DEV, width),...]
where the time goes in v4:
time: 72.9 us; the launch traced here: 72.6 us
  Pallas kernels  68.1 us (93%)
  local copies, waits for them, and re-layouts  3.82 us (5%)
    pallas_call x1, Pallas kernels, on_device(): pl.pallas_call(kernel, out_shape=(jax.ShapeDtypeStruct((NODE_DEV, width),...  66.9 us
    unnamed x8, local copies, waits for them, and re-layouts  3.82 us

profile of v4, /device:TPU:1, one launch (start us, length us, event | category | flops | bytes accessed | tf_op | source)
XLA Modules:
  0.0 72.6 jit_solution(748683608300208135)
XLA Ops:
  0.6 66.9 %shard_map.136 = (bf16[24,6272]{1,0:T(8,128)(2,1)}, bf16[24,6272]{1,0:T(8,128)(2,1)}, bf16[1280,128]{1,0:T(8,128)(2,1)}, bf16[768,128]{1,0:T(8,128)(2,1)}) custom-call(bf16[24,6272]{1,0:T(8,128)(2,1)} %bitcast.5, bf16[768,128]{1,0:T(8,128)(2,1)} %bitcast.7, s32[1,768]{1,0:T(1,128)} %src_ref.1, s32[1,768]{1,0:T(1,128)} %dst_ref.1, bf16[128,128]{1,0:T(8,128)(2,1)} %wq_ref.1, ...), custom_call_target="tpu_custom_call" | custom-call | tf_op jit(solution)/shard_map/pallas_call | solution.py:714
  67.5 0.0 copy-start
  67.5 1.0 %copy-done = bf16[1280,128]{1,0:T(8,128)(2,1)S(1)} copy-done((bf16[1280,128]{1,0:T(8,128)(2,1)S(1)}, bf16[1280,128]{1,0:T(8,128)(2,1)}, u32[]{:S(2)}) %copy-start) | copy-done | bytes 327704
  68.5 0.0 copy-start.1
  68.5 1.0 %copy-done.1 = bf16[24,6272]{1,0:T(8,128)(2,1)S(1)} copy-done((bf16[24,6272]{1,0:T(8,128)(2,1)S(1)}, bf16[24,6272]{1,0:T(8,128)(2,1)}, u32[]{:S(2)}) %copy-start.1) | copy-done | bytes 301080
  69.5 0.0 copy-start.2
  69.5 1.0 %copy-done.2 = bf16[24,6272]{1,0:T(8,128)(2,1)S(1)} copy-done((bf16[24,6272]{1,0:T(8,128)(2,1)S(1)}, bf16[24,6272]{1,0:T(8,128)(2,1)}, u32[]{:S(2)}) %copy-start.2) | copy-done | bytes 301080
  70.4 0.0 copy-start.3
  70.4 0.9 %copy-done.3 = bf16[768,128]{1,0:T(8,128)(2,1)S(1)} copy-done((bf16[768,128]{1,0:T(8,128)(2,1)S(1)}, bf16[768,128]{1,0:T(8,128)(2,1)}, u32[]{:S(2)}) %copy-start.3) | copy-done | bytes 196632
  71.4 1.2 %shard_map.137 = (bf16[24,6272]{1,0:T(8,128)(2,1)}, bf16[24,6272]{1,0:T(8,128)(2,1)}, f32[128,128]{1,0:T(8,128)}, f32[128,128]{1,0:T(8,128)}, f32[128,896]{1,0:T(8,128)}, /*index=5*/f32[7,128,128]{2,1,0:T(8,128)}) custom-call(bf16[24,6272]{1,0:T(8,128)(2,1)S(1)} %copy-done.1, bf16[24,6272]{1,0:T(8,128)(2,1)S(1)} %copy-done.2, bf16[1280,128]{1,0:T(8,128)(2,1)S(1)} %copy-done, ...), custom_call_target="tpu_custom_call" | custom-call | tf_op jit(solution)/shard_map/pallas_call | solution.py:729
Async XLA Ops:
  67.5 1.0 %copy-start = (bf16[1280,128]{1,0:T(8,128)(2,1)S(1)}, bf16[1280,128]{1,0:T(8,128)(2,1)}, u32[]{:S(2)}) copy-start(bf16[1280,128]{1,0:T(8,128)(2,1)} %get-tuple-element.18.ge_ref) | copy-start | bytes 983044
  68.5 1.0 %copy-start.1 = (bf16[24,6272]{1,0:T(8,128)(2,1)S(1)}, bf16[24,6272]{1,0:T(8,128)(2,1)}, u32[]{:S(2)}) copy-start(bf16[24,6272]{1,0:T(8,128)(2,1)} %get-tuple-element.16.u_ref) | copy-start | bytes 903172
  69.5 1.0 %copy-start.2 = (bf16[24,6272]{1,0:T(8,128)(2,1)S(1)}, bf16[24,6272]{1,0:T(8,128)(2,1)}, u32[]{:S(2)}) copy-start(bf16[24,6272]{1,0:T(8,128)(2,1)} %get-tuple-element.17.n_ref) | copy-start | bytes 903172
  70.4 0.9 %copy-start.3 = (bf16[768,128]{1,0:T(8,128)(2,1)S(1)}, bf16[768,128]{1,0:T(8,128)(2,1)}, u32[]{:S(2)}) copy-start(bf16[768,128]{1,0:T(8,128)(2,1)} %get-tuple-element.19.gl_ref) | copy-start | bytes 589828

commit v5 on v4

--- a/solution.py
+++ b/solution.py
@@ -495,8 +495,6 @@
         def _():
             early_second()
 
-    reduce_start(CHUNKS - 1)
-
     early_third()
 
     a = att[...]
@@ -523,6 +521,8 @@
     @pl.loop(1, N_GRAPH)
     def _(d):
         w1_copy(d).start()
+
+    reduce_start(CHUNKS - 1)
 
     back[:, 0:C] = (gm0[...] * scaled[0] + mm_nt(g_key, wk_ref[...])).astype(BF16)
     spread = mm(src_t[...], back[:, 0:C])
@@ -738,7 +738,7 @@
         ),
         in_specs=[vmem] * 4,
         out_specs=(vmem,) * 6,
-        compiler_params=pltpu.CompilerParams(vmem_limit_bytes=32 << 20),
+        compiler_params=pltpu.CompilerParams(vmem_limit_bytes=60 << 20),
     )(updated, grad_node, early, late)
     return (updated[None], grad_node[None], grad_query, grad_key, grad_radial, grad_degree)
 

time: 72.9 us -> 70.1 us (0.962)
  local copies, waits for them, and re-layouts: 3.82 us -> 0 us
  Pallas kernels: 68.1 us -> 69.3 us
    unnamed x8 -> x0, local copies, waits for them, and re-layouts: 3.82 us -> none
    pallas_call x1, Pallas kernels: 1.25 us -> 2.39 us  [on_device(): pl.pallas_call(write_kernel, out_shape=(jax.ShapeDtypeStruct((NODE_DEV, w...]
where the time goes in v5:
time: 70.1 us; the launch traced here: 70 us
  Pallas kernels  69.3 us (99%)
    pallas_call x1, Pallas kernels, on_device(): pl.pallas_call(kernel, out_shape=(jax.ShapeDtypeStruct((NODE_DEV, width),...  66.9 us
    pallas_call x1, Pallas kernels, on_device(): pl.pallas_call(write_kernel, out_shape=(jax.ShapeDtypeStruct((NODE_DEV, w...  2.39 us

profile of v5, /device:TPU:1, one launch (start us, length us, event | category | flops | bytes accessed | tf_op | source)
XLA Modules:
  0.0 70.0 jit_solution(7818825889957063188)
XLA Ops:
  0.6 66.9 %shard_map.136 = (bf16[24,6272]{1,0:T(8,128)(2,1)}, bf16[24,6272]{1,0:T(8,128)(2,1)}, bf16[1280,128]{1,0:T(8,128)(2,1)}, bf16[768,128]{1,0:T(8,128)(2,1)}) custom-call(bf16[24,6272]{1,0:T(8,128)(2,1)} %bitcast.5, bf16[768,128]{1,0:T(8,128)(2,1)} %bitcast.7, s32[1,768]{1,0:T(1,128)} %src_ref.1, s32[1,768]{1,0:T(1,128)} %dst_ref.1, bf16[128,128]{1,0:T(8,128)(2,1)} %wq_ref.1, ...), custom_call_target="tpu_custom_call" | custom-call | tf_op jit(solution)/shard_map/pallas_call | solution.py:714
  67.6 2.4 %shard_map.137 = (bf16[24,6272]{1,0:T(8,128)(2,1)}, bf16[24,6272]{1,0:T(8,128)(2,1)}, f32[128,128]{1,0:T(8,128)}, f32[128,128]{1,0:T(8,128)}, f32[128,896]{1,0:T(8,128)}, /*index=5*/f32[7,128,128]{2,1,0:T(8,128)}) custom-call(bf16[24,6272]{1,0:T(8,128)(2,1)} %get-tuple-element.16.u_ref, bf16[24,6272]{1,0:T(8,128)(2,1)} %get-tuple-element.17.n_ref, ...), custom_call_target="tpu_custom_call" | custom-call | tf_op jit(solution)/shard_map/pallas_call | solution.py:729

commit v6 on v5

--- a/solution.py
+++ b/solution.py
@@ -128,80 +128,6 @@
     x0all[graph, 0:NODE_DEV, :] = x_ref[:, 0:C]
     x0all[graph, NODE_DEV:PAD, :] = jnp.zeros((PAD - NODE_DEV, C), BF16)
 
-    pl.semaphore_wait(barrier, N_GRAPH - 1 + N_DP - 1)
-
-    sib_copy = remote(xs.at[other], sibx, sib_sems.at[0], sib_sems.at[1], sibling)
-    sib_copy.start()
-
-    def x0_copy(d):
-        return remote(
-            x0all.at[graph], x0all.at[graph], x0_send.at[0], x0_recv.at[0],
-            (dp, lax.rem(graph + d, N_GRAPH)),
-        )
-
-    @pl.loop(1, N_GRAPH)
-    def _(d):
-        x0_copy(d).start()
-
-    sib_copy.wait_recv()
-    mine = xs[core, :, 0:NODE_DEV, :].astype(F32)
-    theirs = sibx[:, 0:NODE_DEV, :].astype(F32)
-    first = jnp.where(core == 0, mine, theirs)
-    second = jnp.where(core == 0, theirs, mine)
-    xall[core, :, rows_of(chip), :] = jnp.concatenate([first, second], axis=1).astype(BF16)
-
-    def block(j, which):
-        return xall.at[core, pl.ds(j * CHUNK, CHUNK), rows_of(which), :]
-
-    def gather_copy(j, group, which, device):
-        return lambda: remote(block(j, which), block(j, which), ag_send.at[0], ag_recv.at[j, group], device)
-
-    def gather_first(j):
-        return [
-            gather_copy(j, FIRST, chip, at(1, 0)),
-            gather_copy(j, REST, chip, at(0, 1)),
-            gather_copy(j, REST, chip, at(0, 3)),
-            gather_copy(j, FIRST, chip, at(0, 2)),
-        ]
-
-    def gather_second(j):
-        return [
-            gather_copy(j, REST, chip_at(1, 0), at(0, 1)),
-            gather_copy(j, REST, chip_at(1, 0), at(0, 3)),
-            gather_copy(j, REST, chip_at(0, 2), at(1, 0)),
-        ]
-
-    def to_sibling(j):
-        ref = xall.at[core, pl.ds(j * CHUNK, CHUNK)]
-        return remote(ref, ref, ag_send.at[1], ag_recv.at[j, SIB], sibling)
-
-    def got_blocks(j, group, count):
-        ref = xall.at[core, pl.ds(j * CHUNK, CHUNK), pl.ds(0, count * CHIP_ROWS), :]
-        remote(ref, ref, ag_send.at[0], ag_recv.at[j, group], sibling).wait_recv()
-
-    @pl.loop(0, AHEAD)
-    def _(j):
-        for copy in gather_first(j):
-            copy().start()
-
-    def relay(j):
-        got_blocks(j, FIRST, 2)
-        for copy in gather_second(j):
-            copy().start()
-
-        @pl.when(j + AHEAD < CHUNKS)
-        def _():
-            for copy in gather_first(j + AHEAD):
-                copy().start()
-
-    def forward(j):
-        got_blocks(j, REST, 5)
-        to_sibling(j).start()
-
-    def from_sibling(j):
-        ref = xall.at[other, pl.ds(j * CHUNK, CHUNK)]
-        remote(ref, ref, ag_send.at[1], ag_recv.at[j, SIB], sibling).wait_recv()
-
     src_row = src_ref[...].astype(F32)
     dst_row = (dst_ref[...] - graph * NODE_DEV).astype(F32)
     src_t[...] = (lax.broadcasted_iota(jnp.int32, (NODES, EDGE_DEV), 0).astype(F32) == src_row).astype(F32).astype(BF16)
@@ -210,6 +136,80 @@
     dst_col = jnp.broadcast_to(dst_row, (8, EDGE_DEV)).T[:, 0:1]
     src_hot[...] = (lax.broadcasted_iota(jnp.int32, (EDGE_DEV, NODES), 1).astype(F32) == src_col).astype(F32).astype(BF16)
     dst_hot[...] = (lax.broadcasted_iota(jnp.int32, (EDGE_DEV, PAD), 1).astype(F32) == dst_col).astype(F32).astype(BF16)
+
+    pl.semaphore_wait(barrier, N_GRAPH - 1 + N_DP - 1)
+
+    sib_copy = remote(xs.at[other], sibx, sib_sems.at[0], sib_sems.at[1], sibling)
+    sib_copy.start()
+
+    def x0_copy(d):
+        return remote(
+            x0all.at[graph], x0all.at[graph], x0_send.at[0], x0_recv.at[0],
+            (dp, lax.rem(graph + d, N_GRAPH)),
+        )
+
+    @pl.loop(1, N_GRAPH)
+    def _(d):
+        x0_copy(d).start()
+
+    sib_copy.wait_recv()
+    mine = xs[core, :, 0:NODE_DEV, :].astype(F32)
+    theirs = sibx[:, 0:NODE_DEV, :].astype(F32)
+    first = jnp.where(core == 0, mine, theirs)
+    second = jnp.where(core == 0, theirs, mine)
+    xall[core, :, rows_of(chip), :] = jnp.concatenate([first, second], axis=1).astype(BF16)
+
+    def block(j, which):
+        return xall.at[core, pl.ds(j * CHUNK, CHUNK), rows_of(which), :]
+
+    def gather_copy(j, group, which, device):
+        return lambda: remote(block(j, which), block(j, which), ag_send.at[0], ag_recv.at[j, group], device)
+
+    def gather_first(j):
+        return [
+            gather_copy(j, FIRST, chip, at(1, 0)),
+            gather_copy(j, REST, chip, at(0, 1)),
+            gather_copy(j, REST, chip, at(0, 3)),
+            gather_copy(j, FIRST, chip, at(0, 2)),
+        ]
+
+    def gather_second(j):
+        return [
+            gather_copy(j, REST, chip_at(1, 0), at(0, 1)),
+            gather_copy(j, REST, chip_at(1, 0), at(0, 3)),
+            gather_copy(j, REST, chip_at(0, 2), at(1, 0)),
+        ]
+
+    def to_sibling(j):
+        ref = xall.at[core, pl.ds(j * CHUNK, CHUNK)]
+        return remote(ref, ref, ag_send.at[1], ag_recv.at[j, SIB], sibling)
+
+    def got_blocks(j, group, count):
+        ref = xall.at[core, pl.ds(j * CHUNK, CHUNK), pl.ds(0, count * CHIP_ROWS), :]
+        remote(ref, ref, ag_send.at[0], ag_recv.at[j, group], sibling).wait_recv()
+
+    @pl.loop(0, AHEAD)
+    def _(j):
+        for copy in gather_first(j):
+            copy().start()
+
+    def relay(j):
+        got_blocks(j, FIRST, 2)
+        for copy in gather_second(j):
+            copy().start()
+
+        @pl.when(j + AHEAD < CHUNKS)
+        def _():
+            for copy in gather_first(j + AHEAD):
+                copy().start()
+
+    def forward(j):
+        got_blocks(j, REST, 5)
+        to_sibling(j).start()
+
+    def from_sibling(j):
+        ref = xall.at[other, pl.ds(j * CHUNK, CHUNK)]
+        remote(ref, ref, ag_send.at[1], ag_recv.at[j, SIB], sibling).wait_recv()
 
     rad_t[...] = rad_ref[...].T
     for degree in range(LEVELS):
@@ -542,6 +542,20 @@
     for j in range(CHUNKS - NEXT_LAG, CHUNKS):
         reduce_next(j)
 
+    remote(win1.at[pl.ds(1, N_GRAPH - 1)], win1.at[pl.ds(1, N_GRAPH - 1)], w1_send.at[0], w1_recv.at[0], sibling).wait_recv()
+
+    total = wpart[late_rows(graph), :].astype(F32)
+    for d in range(1, N_GRAPH):
+        total = total + win1[d].astype(F32)
+    win2[dp] = total.astype(BF16)
+
+    def w2_copy(d):
+        return remote(win2.at[dp], win2.at[dp], w2_send.at[0], w2_recv.at[0], (dp_peer(d), graph))
+
+    @pl.loop(1, N_DP)
+    def _(d):
+        w2_copy(d).start()
+
     for degree in range(LEVELS):
         begin, end = degree * degree, (degree + 1) * (degree + 1)
         sums = fwd[begin:end].reshape((end - begin) * NODE_DEV, C).astype(BF16)
@@ -549,20 +563,6 @@
         for k in range(begin, end):
             rows = mixed[(k - begin) * NODE_DEV : (k - begin + 1) * NODE_DEV]
             upd_ref[:, k * C : (k + 1) * C] = (x_ref[:, k * C : (k + 1) * C].astype(F32) + rows).astype(BF16)
-
-    remote(win1.at[pl.ds(1, N_GRAPH - 1)], win1.at[pl.ds(1, N_GRAPH - 1)], w1_send.at[0], w1_recv.at[0], sibling).wait_recv()
-
-    total = wpart[late_rows(graph), :].astype(F32)
-    for d in range(1, N_GRAPH):
-        total = total + win1[d].astype(F32)
-    win2[dp] = total.astype(BF16)
-
-    def w2_copy(d):
-        return remote(win2.at[dp], win2.at[dp], w2_send.at[0], w2_recv.at[0], (dp_peer(d), graph))
-
-    @pl.loop(1, N_DP)
-    def _(d):
-        w2_copy(d).start()
 
     early_fifth()
     for j in range(CHUNKS - END_LAG, CHUNKS - 1):

time: 70.1 us -> 70 us (level)
  no operation moved by 1% of the time
where the time goes in v6:
time: 70 us; the launch traced here: 69.9 us
  Pallas kernels  69.2 us (99%)
    pallas_call x1, Pallas kernels, on_device(): pl.pallas_call(kernel, out_shape=(jax.ShapeDtypeStruct((NODE_DEV, width),...  66.8 us
    pallas_call x1, Pallas kernels, on_device(): pl.pallas_call(write_kernel, out_shape=(jax.ShapeDtypeStruct((NODE_DEV, w...  2.39 us

profile of v6, /device:TPU:1, one launch (start us, length us, event | category | flops | bytes accessed | tf_op | source)
XLA Modules:
  0.0 69.9 jit_solution(1314655517942883498)
XLA Ops:
  0.6 66.8 %shard_map.136 = (bf16[24,6272]{1,0:T(8,128)(2,1)}, bf16[24,6272]{1,0:T(8,128)(2,1)}, bf16[1280,128]{1,0:T(8,128)(2,1)}, bf16[768,128]{1,0:T(8,128)(2,1)}) custom-call(bf16[24,6272]{1,0:T(8,128)(2,1)} %bitcast.5, bf16[768,128]{1,0:T(8,128)(2,1)} %bitcast.7, s32[1,768]{1,0:T(1,128)} %src_ref.1, s32[1,768]{1,0:T(1,128)} %dst_ref.1, bf16[128,128]{1,0:T(8,128)(2,1)} %wq_ref.1, ...), custom_call_target="tpu_custom_call" | custom-call | tf_op jit(solution)/shard_map/pallas_call | solution.py:714
  67.5 2.4 %shard_map.137 = (bf16[24,6272]{1,0:T(8,128)(2,1)}, bf16[24,6272]{1,0:T(8,128)(2,1)}, f32[128,128]{1,0:T(8,128)}, f32[128,128]{1,0:T(8,128)}, f32[128,896]{1,0:T(8,128)}, /*index=5*/f32[7,128,128]{2,1,0:T(8,128)}) custom-call(bf16[24,6272]{1,0:T(8,128)(2,1)} %get-tuple-element.16.u_ref, bf16[24,6272]{1,0:T(8,128)(2,1)} %get-tuple-element.17.n_ref, ...), custom_call_target="tpu_custom_call" | custom-call | tf_op jit(solution)/shard_map/pallas_call | solution.py:729
